TPU v7x, 32 devices: a whole 2x2x4 slice. The times are simulated.
32 devices in a mesh: tm: 8 (over z, core), blk: 4 (over y, x).
Axes of the slice: x: 2, y: 2, z: 4, core: 2. Of those that a mesh axis runs over, the one named last changes fastest.
Arguments:
- queries: bfloat16 [32, 9, 3840], P('blk'), may hold values from -6 to 6
- index_regions: bfloat16 [4, 9, 512, 3840], P('blk', None, 'tm'), may hold values from -0.09375 to 0.09375
- conv_one: float32 [16, 9], replicated, may hold values from -2 to 2
- bias_one: float32 [16], replicated, may hold values from -3 to 3
- conv_two: float32 [16, 9], replicated, may hold values from -0.5 to 0.5
- bias_two: float32 [1], replicated, may hold values from -3 to 3
- index_lengths: int32 [4, 8], P('blk'), may hold values from 1 to 128, 512 in all within a row
- query_lengths: int32 [4], replicated, may hold values from 1 to 16, 32 in all
Outputs:
- scores: float32 [4, 4, 8], P('blk')
Inputs may be any that keep to these rules, and one draw needn't show every extreme that they name: Each row of index_lengths lists the frame counts of the index videos of one partition in time order; they sum to 512, and some video has exactly 128 frames. query_lengths lists the frame counts of the query clips in time order; they sum to 32, and some clip has exactly 16 frames.
All inputs are finite; a program needn't handle non-finite values.
Results may differ from a plain program's by a relative error of at most 0.0003.
Values may be sent and summed in bfloat16 or wider, within the bound.
No kernel may reach another device: no remote copies, remote signals or barrier semaphores. Data moves between devices by JAX's collectives and lax.ppermute only.
A program may use at most 64 MiB of HBM per device.

v0:
```python
import jax
import jax.numpy as jnp
from jax import lax
from jax.sharding import PartitionSpec as P

very_low = -1000000000.0
highest = lax.Precision.HIGHEST


def padded(x, sides, width):
    for axis, dim in sides:
        size, length = (lax.axis_size(axis), x.shape[dim])
        up = [(i, (i + 1) % size) for i in range(size - 1)]
        down = [(j, i) for i, j in up]
        last = lax.slice_in_dim(x, length - width, length, axis=dim)
        first = lax.slice_in_dim(x, 0, width, axis=dim)
        before = lax.ppermute(last, axis, up)
        after = lax.ppermute(first, axis, down)
        x = jnp.concatenate([before, x, after], axis=dim)
    return x


def from_behind(block, axis, distance):
    devices = range(lax.axis_size(axis))
    route = [((i - distance) % len(devices), i) for i in devices]
    return lax.ppermute(block, axis, route)


def segment_ids(lengths, positions, extent):
    starts = jnp.cumsum(lengths) - lengths
    inside = (positions >= 0) & (positions < extent)
    counts = jnp.sum((positions[:, None] >= starts[None, :]).astype(jnp.int32), axis=1) - 1
    return jnp.where(inside, counts, -1)


def frame_similarity(block, index_rows):
    row_count, regions, feature_width = block.shape
    col_count = index_rows.shape[1]
    products = lax.dot_general(
        block.reshape(row_count * regions, feature_width),
        index_rows.reshape(regions * col_count, feature_width),
        (((1,), (1,)), ((), ())),
        preferred_element_type=jnp.float32,
    )
    products = products.reshape(row_count, regions, regions, col_count)
    return jnp.mean(jnp.max(products, axis=2), axis=1)


def neighbour_masks(ids, extent):
    centre = ids[1 : extent + 1]
    return [
        ((ids[shift_by : shift_by + extent] == centre) & (centre >= 0)).astype(jnp.float32)
        for shift_by in range(3)
    ]


def stencil_taps(source, row_ids, col_ids):
    height = source.shape[-2] - 2
    breadth = source.shape[-1] - 2
    row_masks = neighbour_masks(row_ids, height)
    col_masks = neighbour_masks(col_ids, breadth)
    shifted = []
    for row_step in range(3):
        for col_step in range(3):
            window = source[..., row_step : row_step + height, col_step : col_step + breadth]
            shifted.append(window * (row_masks[row_step][:, None] * col_masks[col_step][None, :]))
    return jnp.stack(shifted)


def refine(similar, row_ids, col_ids, conv_one, bias_one, conv_two, bias_two):
    shifted = stencil_taps(similar, row_ids, col_ids)
    hidden = (
        jnp.einsum("ct,tij->cij", conv_one, shifted, precision=highest) + bias_one[:, None, None]
    )
    hidden = jax.nn.relu(hidden)
    shifted = stencil_taps(hidden, row_ids[1:-1], col_ids[1:-1])
    return jnp.einsum("ct,tcij->ij", conv_two, shifted, precision=highest) + bias_two[0]


def shards(
    queries, index_regions, conv_one, bias_one, conv_two, bias_two, index_lengths, query_lengths
):
    cycle_size = lax.axis_size("blk")
    cycle_pos = lax.axis_index("blk")
    time_size = lax.axis_size("tm")
    block_rows = queries.shape[0]
    total_rows = block_rows * cycle_size
    local_index = index_regions[0]
    frames = local_index.shape[1]
    video_lengths = index_lengths[0]
    videos = video_lengths.shape[0]
    first_frame = lax.axis_index("tm") * frames
    col_ids = segment_ids(
        video_lengths, first_frame - 2 + jnp.arange(frames + 4, dtype=jnp.int32), frames * time_size
    )
    holders = col_ids[2:-2][:, None] == jnp.arange(videos, dtype=jnp.int32)[None, :]
    wide_index = padded(local_index, (("tm", 1),), 2)

    def similar_wide(block):
        return frame_similarity(block, wide_index)

    def video_maxima(block, first_row):
        row_count = block.shape[0] - 4
        row_ids = segment_ids(
            query_lengths, first_row - 2 + jnp.arange(row_count + 4, dtype=jnp.int32), total_rows
        )
        refined = refine(
            similar_wide(block), row_ids, col_ids, conv_one, bias_one, conv_two, bias_two
        )
        return jnp.max(jnp.where(holders[None, :, :], refined[:, :, None], very_low), axis=1)

    def record(video_table, block, owner_block):
        first_row = owner_block * block_rows
        return lax.dynamic_update_slice_in_dim(
            video_table, video_maxima(block, first_row), first_row, 0
        )

    query_block = padded(queries, (("blk", 0),), 2)
    video_table = jnp.zeros((total_rows, videos), jnp.float32)
    video_table = record(video_table, query_block, cycle_pos)
    for cycle_step in range(1, cycle_size):
        query_block = from_behind(query_block, "blk", 1)
        video_table = record(video_table, query_block, (cycle_pos - cycle_step) % cycle_size)
    global_max = lax.pmax(video_table, "tm")
    clip_ids = segment_ids(query_lengths, jnp.arange(total_rows, dtype=jnp.int32), total_rows)
    clip_count = query_lengths.shape[0]
    members = (jnp.arange(clip_count, dtype=jnp.int32)[:, None] == clip_ids[None, :]).astype(
        jnp.float32
    )
    totals = jnp.dot(members, global_max, precision=highest, preferred_element_type=jnp.float32)
    scores = totals / query_lengths.astype(jnp.float32)[:, None]
    return scores[None]


def solution(mesh):
    placed = (
        P("blk", None, None),
        P("blk", None, "tm", None),
        P(),
        P(),
        P(),
        P(),
        P("blk", None),
        P(),
    )
    return jax.shard_map(
        shards, mesh=mesh, in_specs=placed, out_specs=P("blk", None, None), check_vma=False
    )
```

profile of v0, /device:TPU:0, one launch (start us, length us, event | category | flops | bytes accessed | tf_op | source)
XLA Modules:
  0.0 149.1 jit_solution(11066358805916678227)
XLA Ops:
  0.0 1.4 fusion.102
  1.5 2.4 %collective-permute-start.2 = (bf16[9,2,3840]{2,1,0:T(2,128)(2,1)S(1)}, bf16[9,2,3840]{2,1,0:T(2,128)(2,1)S(1)}, u32[]{:S(2)}, u32[]{:S(2)}) collective-permute-start(bf16[9,2,3840]{2,1,0:T(2,128)(2,1)S(1)} %get-tuple-element.13), channel_id=1, source_target_pairs={{0,4},{4,8},{8,12},{12,16},{16,20},{20,24},{24,28},{1,5},{5,9},{9,... | collective-permute-start | bytes 414728 | tf_op jit(solution)/shard_map/ppermute | solution.py:17
  3.8 1.3 collective-permute-start.3
  5.1 1.4 fusion.103
  6.6 4.2 %collective-permute-start = (bf16[2,9,3840]{2,0,1:T(2,128)(2,1)S(1)}, bf16[2,9,3840]{2,0,1:T(2,128)(2,1)S(1)}, u32[]{:S(2)}, u32[]{:S(2)}) collective-permute-start(bf16[2,9,3840]{2,0,1:T(2,128)(2,1)S(1)} %get-tuple-element.15), channel_id=1, source_target_pairs={{0,1},{1,2},{2,3},{4,5},{5,6},{6,7},{8,9},{9,10},{10,11},{12,13},{... | collective-permute-start | bytes 414728 | tf_op jit(solution)/shard_map/ppermute | solution.py:17
  10.8 1.3 collective-permute-start.1
  12.2 0.8 reduce-window_1_clone.1
  13.0 0.7 subtract_bitcast_fusion
  14.0 0.8 reduce-window.10
  14.8 0.7 fusion.104
  16.9 0.8 copy.43
  17.9 1.2 collective-permute-done.1
  19.0 5.3 %convolution_reduce_fusion.3 = f32[12,9,68]{2,0,1:T(8,128)S(1)} fusion(bf16[2,9,3840]{2,0,1:T(2,128)(2,1)S(1)} %collective-permute-done.1, bf16[8,9,3840]{2,0,1:T(8,128)(2,1)} %param.8, bf16[2,9,3840]{2,0,1:T(2,128)(2,1)S(1)} %collective-permute-done, bf16[9,2,3840]{2,1,0:T(2,128)(2,1)S(1)} %collective-permute-done.3, bf16[9,64,3840]{2,1,0:T(8,128)(2,1)} %bitcast.348, ...), kind=kOutput, calls=%fused_computation.4 | convolution fusion | flops 524264832 | bytes 5558976 | tf_op jit(solution)/shard_map/dot_general | solution.py:39
  24.6 0.5 pad_maximum_fusion
  25.1 1.6 %collective-permute-start.4 = (bf16[12,9,3840]{2,0,1:T(8,128)(2,1)S(1)}, bf16[12,9,3840]{2,0,1:T(8,128)(2,1)}, u32[]{:S(2)}, u32[]{:S(2)}) collective-permute-start(bf16[12,9,3840]{2,0,1:T(8,128)(2,1)S(1)} %pad_maximum_fusion), channel_id=1, source_target_pairs={{3,0},{0,1},{1,2},{2,3},{7,4},{4,5},{5,6},{6,7},{11,8},{8,9},{9,10... | collective-permute-start | bytes 2488328 | tf_op jit(solution)/shard_map/ppermute | solution.py:26
  27.6 25.1 %collective-permute-done.4 = bf16[12,9,3840]{2,0,1:T(8,128)(2,1)} collective-permute-done((bf16[12,9,3840]{2,0,1:T(8,128)(2,1)S(1)}, bf16[12,9,3840]{2,0,1:T(8,128)(2,1)}, u32[]{:S(2)}, u32[]{:S(2)}) %collective-permute-start.4) | collective-permute-done | bytes 829472 | tf_op jit(solution)/shard_map/ppermute | solution.py:26
  52.7 0.5 collective-permute-start.5
  53.1 0.4 fusion.105
  53.6 5.2 %convolution_reduce_fusion.2 = f32[12,9,68]{2,0,1:T(8,128)S(1)} fusion(bf16[12,9,3840]{2,0,1:T(8,128)(2,1)} %collective-permute-done.4, bf16[9,2,3840]{2,1,0:T(2,128)(2,1)S(1)} %collective-permute-done.3, bf16[9,64,3840]{2,1,0:T(8,128)(2,1)} %bitcast.349, bf16[9,2,3840]{2,1,0:T(2,128)(2,1)S(1)} %collective-permute-done.2), kind=kOutput, calls=%fused_computation.3 | convolution fusion | flops 521776512 | bytes 5558976 | tf_op jit(solution)/shard_map/dot_general | solution.py:39
  58.8 21.9 %collective-permute-done.5 = bf16[12,9,3840]{2,0,1:T(8,128)(2,1)S(1)} collective-permute-done((bf16[12,9,3840]{2,0,1:T(8,128)(2,1)}, bf16[12,9,3840]{2,0,1:T(8,128)(2,1)S(1)}, u32[]{:S(2)}, u32[]{:S(2)}) %collective-permute-start.5) | collective-permute-done | bytes 829472 | tf_op jit(solution)/shard_map/ppermute | solution.py:26
  80.6 4.8 %convolution_reduce_fusion.1 = f32[12,9,68]{2,0,1:T(8,128)S(1)} fusion(bf16[12,9,3840]{2,0,1:T(8,128)(2,1)S(1)} %collective-permute-done.5, bf16[9,2,3840]{2,1,0:T(2,128)(2,1)S(1)} %collective-permute-done.3, bf16[9,64,3840]{2,1,0:T(8,128)(2,1)} %bitcast.350, bf16[9,2,3840]{2,1,0:T(2,128)(2,1)S(1)} %collective-permute-done.2), kind=kOutput, calls=%fused_computation.2 | convolution fusion | flops 521776512 | bytes 5558976 | tf_op jit(solution)/shard_map/dot_general | solution.py:39
  85.7 0.7 collective-permute-start.6
  86.7 26.1 %collective-permute-done.6 = bf16[12,9,3840]{2,0,1:T(8,128)(2,1)S(1)} collective-permute-done((bf16[12,9,3840]{2,0,1:T(8,128)(2,1)S(1)}, bf16[12,9,3840]{2,0,1:T(8,128)(2,1)S(1)}, u32[]{:S(2)}, u32[]{:S(2)}) %collective-permute-start.6) | collective-permute-done | bytes 829472 | tf_op jit(solution)/shard_map/ppermute | solution.py:26
  112.8 4.8 %convolution_reduce_fusion = f32[12,9,68]{2,0,1:T(8,128)S(1)} fusion(bf16[12,9,3840]{2,0,1:T(8,128)(2,1)S(1)} %collective-permute-done.6, bf16[9,2,3840]{2,1,0:T(2,128)(2,1)S(1)} %collective-permute-done.3, bf16[9,64,3840]{2,1,0:T(8,128)(2,1)} %bitcast.351, bf16[9,2,3840]{2,1,0:T(2,128)(2,1)S(1)} %collective-permute-done.2), kind=kOutput, calls=%fused_computation.1 | convolution fusion | flops 521776512 | bytes 5558976 | tf_op jit(solution)/shard_map/dot_general | solution.py:39
  117.9 0.2 fusion.3
  118.6 0.2 fusion.5
  119.0 0.2 fusion.1
  119.8 0.4 fusion.108
  120.9 0.4 fusion.106
  121.9 0.4 fusion.107
  122.5 25.9 %pmax.7 = f32[32,8]{1,0:T(8,128)S(1)} all-reduce(f32[32,8]{1,0:T(8,128)S(1)} %constant_dynamic-update-slice_fusion.63), channel_id=1, replica_groups=mesh['tm'=8,'blk'=4] {'tm'}, use_global_device_ids=true, to_apply=%region_20.21 | all-reduce | flops 256 | bytes 2048 | tf_op jit(solution)/shard_map/pmax | solution.py:124
  148.4 0.7 fusion.8
  (117 shorter events, 5.2 us)
Async XLA Ops:
  0.0 26.8 %copy-start = (f32[16,9]{1,0:T(8,128)S(1)}, f32[16,9]{1,0:T(8,128)}, u32[]{:S(2)}) copy-start(f32[16,9]{1,0:T(8,128)} %param.10) | copy-start | bytes 1732
  1.5 16.4 %collective-permute-start.2 = (bf16[9,2,3840]{2,1,0:T(2,128)(2,1)S(1)}, bf16[9,2,3840]{2,1,0:T(2,128)(2,1)S(1)}, u32[]{:S(2)}, u32[]{:S(2)}) collective-permute-start(bf16[9,2,3840]{2,1,0:T(2,128)(2,1)S(1)} %get-tuple-element.13), channel_id=1, source_target_pairs={{0,4},{4,8},{8,12},{12,16},{16,20},{20,24},{24,28},{1,5},{5,9},{9,... | collective-permute-start | bytes 414728 | tf_op jit(solution)/shard_map/ppermute | solution.py:17
  3.8 14.0 %collective-permute-start.3 = (bf16[9,2,3840]{2,1,0:T(2,128)(2,1)S(1)}, bf16[9,2,3840]{2,1,0:T(2,128)(2,1)S(1)}, u32[]{:S(2)}, u32[]{:S(2)}) collective-permute-start(bf16[9,2,3840]{2,1,0:T(2,128)(2,1)S(1)} %get-tuple-element.14), channel_id=1, source_target_pairs={{4,0},{8,4},{12,8},{16,12},{20,16},{24,20},{28,24},{5,1},{9,5},{13... | collective-permute-start | bytes 414728 | tf_op jit(solution)/shard_map/ppermute | solution.py:18
  6.6 11.3 %collective-permute-start = (bf16[2,9,3840]{2,0,1:T(2,128)(2,1)S(1)}, bf16[2,9,3840]{2,0,1:T(2,128)(2,1)S(1)}, u32[]{:S(2)}, u32[]{:S(2)}) collective-permute-start(bf16[2,9,3840]{2,0,1:T(2,128)(2,1)S(1)} %get-tuple-element.15), channel_id=1, source_target_pairs={{0,1},{1,2},{2,3},{4,5},{5,6},{6,7},{8,9},{9,10},{10,11},{12,13},{... | collective-permute-start | bytes 414728 | tf_op jit(solution)/shard_map/ppermute | solution.py:17
  10.8 8.2 %collective-permute-start.1 = (bf16[2,9,3840]{2,0,1:T(2,128)(2,1)S(1)}, bf16[2,9,3840]{2,0,1:T(2,128)(2,1)S(1)}, u32[]{:S(2)}, u32[]{:S(2)}) collective-permute-start(bf16[2,9,3840]{2,0,1:T(2,128)(2,1)S(1)} %get-tuple-element.16), channel_id=1, source_target_pairs={{1,0},{2,1},{3,2},{5,4},{6,5},{7,6},{9,8},{10,9},{11,10},{13,12},{... | collective-permute-start | bytes 414728 | tf_op jit(solution)/shard_map/ppermute | solution.py:18
  17.8 6.8 %copy-start.1 = (bf16[8,9,3840]{2,0,1:T(8,128)(2,1)S(1)}, bf16[8,9,3840]{2,0,1:T(8,128)(2,1)}, u32[]{:S(2)}) copy-start(bf16[8,9,3840]{2,0,1:T(8,128)(2,1)} %param.8) | copy-start | bytes 1658884
  17.8 8.9 %copy-start.2 = (f32[16]{0:T(128)S(1)}, f32[16]{0:T(128)}, u32[]{:S(2)}) copy-start(f32[16]{0:T(128)} %param.11) | copy-start | bytes 196
  25.1 27.6 %collective-permute-start.4 = (bf16[12,9,3840]{2,0,1:T(8,128)(2,1)S(1)}, bf16[12,9,3840]{2,0,1:T(8,128)(2,1)}, u32[]{:S(2)}, u32[]{:S(2)}) collective-permute-start(bf16[12,9,3840]{2,0,1:T(8,128)(2,1)S(1)} %pad_maximum_fusion), channel_id=1, source_target_pairs={{3,0},{0,1},{1,2},{2,3},{7,4},{4,5},{5,6},{6,7},{11,8},{8,9},{9,10... | collective-permute-start | bytes 2488328 | tf_op jit(solution)/shard_map/ppermute | solution.py:26
  52.7 28.0 %collective-permute-start.5 = (bf16[12,9,3840]{2,0,1:T(8,128)(2,1)}, bf16[12,9,3840]{2,0,1:T(8,128)(2,1)S(1)}, u32[]{:S(2)}, u32[]{:S(2)}) collective-permute-start(bf16[12,9,3840]{2,0,1:T(8,128)(2,1)} %collective-permute-done.4), channel_id=1, source_target_pairs={{3,0},{0,1},{1,2},{2,3},{7,4},{4,5},{5,6},{6,7},{11,8},{8,9},{9,10... | collective-permute-start | bytes 2488328 | tf_op jit(solution)/shard_map/ppermute | solution.py:26
  85.7 27.1 %collective-permute-start.6 = (bf16[12,9,3840]{2,0,1:T(8,128)(2,1)S(1)}, bf16[12,9,3840]{2,0,1:T(8,128)(2,1)S(1)}, u32[]{:S(2)}, u32[]{:S(2)}) collective-permute-start(bf16[12,9,3840]{2,0,1:T(8,128)(2,1)S(1)} %collective-permute-done.5), channel_id=1, source_target_pairs={{3,0},{0,1},{1,2},{2,3},{7,4},{4,5},{5,6},{6,7},{11,8},{8,9},{9,10... | collective-permute-start | bytes 2488328 | tf_op jit(solution)/shard_map/ppermute | solution.py:26
where the time goes:
time: 150 us; the launch traced here: 149 us
  waiting for transfers between devices  74.3 us (50%)
  blocking collectives  25.9 us (17%)
  matrix products  23.3 us (16%)
  starting transfers between devices  11.9 us (8%)
  other arithmetic  8.28 us (6%)
  local copies, waits for them, and re-layouts  3.94 us (3%)
    ppermute x3, waiting for transfers between devices, from_behind(): return lax.ppermute(block, axis, route)  73.1 us
    pmax x1, blocking collectives, shards(): global_max = lax.pmax(video_table, 'tm')  25.9 us
    dot_general x4, matrix products, frame_similarity(): lax.dot_general(block.reshape(row_count * regions, feature_width), index_...  20.1 us
    ppermute x2, starting transfers between devices, padded(): before = lax.ppermute(last, axis, up)  6.6 us
  transfers between devices with their start and end apart: 7, of which 4 were waited for; matrix products, arithmetic and copies ran while one was open for 9% of the time, Pallas kernels for 0%

commit v1 on v0

v1 whole, which is shorter than its diff:
```python
import functools
import jax
import jax.numpy as jnp
from jax import lax
from jax.experimental import pallas as pl
from jax.experimental.pallas import tpu as pltpu
from jax.sharding import PartitionSpec as P

very_low = -1000000000.0
highest = lax.Precision.HIGHEST
LANES = 128
SUBLANES = 8
VMEM_LIMIT = 32 * 1024 * 1024


def inner(a, b, precision=None):
    return lax.dot_general(
        a, b, (((1,), (1,)), ((), ())), precision=precision, preferred_element_type=jnp.float32
    )


def stacked(refs):
    return refs[0][...] if len(refs) == 1 else jnp.concatenate([r[...] for r in refs], axis=0)


def region_maxima(index_ref, outside_ref, inside_ref, parts, parity):
    regions, frames, _ = index_ref.shape
    own = None
    border = None
    for first, size, refs in parts:
        block = stacked(refs)
        at = pl.ds(first, size)
        rows = index_ref[:, :, at].reshape(regions * frames, size)
        ends = jnp.concatenate([outside_ref[:, at], inside_ref[:, at]], axis=0)
        products = inner(rows, block)
        sides = inner(ends, block)
        own = products if own is None else own + products
        border = sides if border is None else border + sides
    width = own.shape[1]
    maxima = jnp.max(own.reshape(regions, frames, width), axis=0)
    row = lax.broadcasted_iota(jnp.int32, border.shape, 0)
    count = 2 * regions

    def end_max(side, j):
        picked = (row >= side * count) & (row < (side + 1) * count) & (row % 2 == j)
        return jnp.max(jnp.where(picked, border, -jnp.inf), axis=0, keepdims=True)

    ends = [[end_max(side, j) for j in range(2)] for side in range(2)]
    even = parity == 0
    after = [jnp.where(even, ends[1][j], ends[0][j]) for j in range(2)]
    before = [jnp.where(even, ends[0][j], ends[1][j]) for j in range(2)]
    slot = lax.broadcasted_iota(jnp.int32, (SUBLANES, width), 0)
    last = jnp.zeros((SUBLANES, width), jnp.float32)
    for place, value in ((0, after[0]), (1, after[1]), (6, before[0]), (7, before[1])):
        last = jnp.where(slot == place, value, last)
    return maxima, last


def region_mean(maxima, last, blocks, block_rows, regions, total_rows):
    frames, width = maxima.shape
    gap = jnp.zeros((LANES - frames - 2 * SUBLANES, width), jnp.float32)
    table = jnp.concatenate([maxima, last, gap, last], axis=0)
    row = lax.broadcasted_iota(jnp.int32, (total_rows, width), 0)
    lane = lax.broadcasted_iota(jnp.int32, (total_rows, width), 1)
    per_block = regions * block_rows
    picked = jnp.zeros((total_rows, width), jnp.bool_)
    for number, block in enumerate(blocks):
        inside = (lane >= number * per_block) & (lane < (number + 1) * per_block)
        picked = picked | (inside & (row == block * block_rows + lane % block_rows))
    return inner(picked.astype(jnp.float32), table, highest)


def ids_at(lengths, count, positions):
    found = jnp.full(positions.shape, -1, jnp.int32)
    start = jnp.int32(0)
    for k in range(count):
        found = found + (positions >= start).astype(jnp.int32)
        start = start + lengths(k)
    return found


def refine_and_best(
    similar, first_frame, extent, frames, video_ref, clip_ref, one_ref, bias_one_ref, two_ref, bias_two_ref
):
    total_rows = similar.shape[0]
    channels = bias_one_ref.shape[0]
    videos = video_ref.shape[1]
    shape = (total_rows, LANES)
    lane = lax.broadcasted_iota(jnp.int32, shape, 1)
    row = lax.broadcasted_iota(jnp.int32, shape, 0)
    offset = jnp.where(lane < frames + SUBLANES, lane, lane - LANES)
    position = first_frame + offset
    known = (offset >= -2) & (offset < frames + 2) & (position >= 0) & (position < extent)
    col_ids = jnp.where(known, ids_at(lambda k: video_ref[0, k], videos, position), -1)
    row_ids = ids_at(lambda k: clip_ref[k], clip_ref.shape[0], row)

    def rolled(x, step, axis):
        return x if step == 0 else pltpu.roll(x, (-step) % x.shape[axis], axis)

    steps = (-1, 0, 1)
    col_mask = [
        ((rolled(col_ids, b, 1) == col_ids) & (col_ids >= 0)).astype(jnp.float32) for b in steps
    ]
    row_mask = [
        (
            (rolled(row_ids, a, 0) == row_ids) & (row + a >= 0) & (row + a < total_rows)
        ).astype(jnp.float32)
        for a in steps
    ]
    across = [rolled(similar, b, 1) * col_mask[b + 1] for b in steps]
    taps = []
    for a in steps:
        for b in steps:
            tap = across[b + 1]
            taps.append(tap if a == 0 else rolled(tap, a, 0) * row_mask[a + 1])
    piece = 2 * SUBLANES
    gathered = [[] for _ in range(9)]
    for top in range(0, total_rows, piece):
        source = [tap[top : top + piece] for tap in taps]
        sums = [None] * 9
        for c in range(channels):
            hidden = one_ref[c, 0] * source[0] + bias_one_ref[c]
            for t in range(1, 9):
                hidden = hidden + one_ref[c, t] * source[t]
            hidden = jnp.maximum(hidden, 0.0)
            for t in range(9):
                term = two_ref[c, t] * hidden
                sums[t] = term if c == 0 else sums[t] + term
        for t in range(9):
            gathered[t].append(sums[t])
    gathered = [jnp.concatenate(parts, axis=0) for parts in gathered]
    refined = jnp.full(shape, bias_two_ref[0], jnp.float32)
    for b in steps:
        column = gathered[3 + b + 1]
        for a in (-1, 1):
            column = column + rolled(gathered[3 * (a + 1) + b + 1], a, 0) * row_mask[a + 1]
        refined = refined + rolled(column, b, 1) * col_mask[b + 1]
    own_ids = jnp.where((offset >= 0) & (offset < frames), col_ids, -1)
    best = jnp.full(shape, very_low, jnp.float32)
    for v in range(videos):
        top_value = jnp.max(
            jnp.where(own_ids == v, refined, very_low), axis=1, keepdims=True
        )
        best = jnp.where(lane == v, top_value, best)
    return best[:, :videos]


def parts_of(layout, refs, parity, depth):
    half = depth // 2
    parts = []
    taken = 0
    for which, count in layout:
        pieces = refs[taken : taken + count]
        taken += count
        if which is None:
            parts.append((0, depth, pieces))
        else:
            side = parity if which == 0 else 1 - parity
            parts.append((pl.multiple_of(side * half, LANES), half, pieces))
    return parts


def early_kernel(layout, index_ref, outside_ref, inside_ref, *refs):
    *pieces, maxima_ref, last_ref = refs
    parity = lax.axis_index("tm") % 2
    parts = parts_of(layout, pieces, parity, index_ref.shape[2])
    maxima, last = region_maxima(index_ref, outside_ref, inside_ref, parts, parity)
    maxima_ref[...] = maxima
    last_ref[...] = last


def late_kernel(
    layout, blocks_of, early_of, block_rows, total_rows, extent,
    video_ref, clip_ref, one_ref, bias_one_ref, two_ref, bias_two_ref,
    index_ref, outside_ref, inside_ref, *refs,
):
    *refs, best_ref = refs
    regions, frames, depth = index_ref.shape
    time_index = lax.axis_index("tm")
    parity = time_index % 2
    position = lax.axis_index("blk")
    early = 0 if early_of is None else 2
    parts = parts_of(layout, refs[early:], parity, depth)
    maxima, last = region_maxima(index_ref, outside_ref, inside_ref, parts, parity)
    mean_of = functools.partial(
        region_mean, block_rows=block_rows, regions=regions, total_rows=total_rows
    )
    similar = mean_of(maxima, last, blocks_of(parity, position))
    if early:
        similar = similar + mean_of(refs[0][...], refs[1][...], early_of(parity, position))
    similar = similar * (1.0 / regions)
    best_ref[...] = refine_and_best(
        similar, time_index * frames, extent, frames,
        video_ref, clip_ref, one_ref, bias_one_ref, two_ref, bias_two_ref,
    )


def score_kernel(clip_ref, *refs):
    *tables, scores_ref = refs
    best = tables[0][...]
    for table in tables[1:]:
        best = jnp.maximum(best, table[...])
    rows = best.shape[0]
    clips = clip_ref.shape[0]
    row_ids = ids_at(lambda k: clip_ref[k], clips, lax.broadcasted_iota(jnp.int32, best.shape, 0))
    for c in range(clips):
        total = jnp.sum(jnp.where(row_ids == c, best, 0.0), axis=0, keepdims=True)
        scores_ref[0, c : c + 1, :] = total / clip_ref[c].astype(jnp.float32)


def in_vmem():
    return pl.BlockSpec(memory_space=pltpu.VMEM)


def in_smem():
    return pl.BlockSpec(memory_space=pltpu.SMEM)


def shards(
    queries, index_regions, conv_one, bias_one, conv_two, bias_two, index_lengths, query_lengths
):
    cycle_size = lax.axis_size("blk")
    time_size = lax.axis_size("tm")
    block_rows, regions, depth = queries.shape
    total_rows = block_rows * cycle_size
    index = index_regions[0]
    frames = index.shape[1]
    extent = frames * time_size
    videos = index_lengths.shape[1]
    odd = lax.axis_index("tm") % 2 == 1
    half = depth // 2
    width = regions * block_rows

    def sent(x, source):
        pairs = []
        for t in range(time_size):
            for b in range(cycle_size):
                found = source(t, b)
                if found is not None and 0 <= found[0] < time_size:
                    pairs.append((found[0] * cycle_size + found[1], t * cycle_size + b))
        return lax.ppermute(x, ("tm", "blk"), pairs)

    def beside(t, b):
        return t ^ 1, b

    def crossing(t, b):
        return (t - 1, b) if t % 2 == 0 else (t + 1, b)

    def ends():
        head = index[:, :2].reshape(2 * regions, depth)
        tail = index[:, frames - 2 :].reshape(2 * regions, depth)
        outer = jnp.where(odd, tail, head)
        inner_side = jnp.where(odd, head, tail)
        return sent(outer, crossing), sent(inner_side, beside)

    flat = jnp.swapaxes(queries, 0, 1).reshape(width, depth)
    scalars = (index_lengths, query_lengths, conv_one, bias_one, conv_two, bias_two)
    params = pltpu.CompilerParams(vmem_limit_bytes=VMEM_LIMIT)
    if cycle_size == 4:
        first = jnp.where(odd, flat[:, :half], flat[:, half:])
        second = jnp.where(odd, flat[:, half:], flat[:, :half])

        def near(t, b):
            return (t, b ^ 1) if t % 2 == 0 else (t, b ^ 2)

        def far(t, b):
            return (t ^ 1, b ^ 1) if t % 2 == 0 else (t ^ 1, b ^ 2)

        near_first = sent(first, near)
        near_second = sent(second, near)
        outside, inside = ends()
        far_first = sent(near_first, far)
        next_first = sent(near_first, beside)
        next_second = sent(near_second, beside)
        early = pl.pallas_call(
            functools.partial(early_kernel, ((1, 2), (0, 2))),
            in_specs=[in_vmem()] * 7,
            out_specs=[in_vmem()] * 2,
            out_shape=[
                jax.ShapeDtypeStruct((frames, 2 * width), jnp.float32),
                jax.ShapeDtypeStruct((SUBLANES, 2 * width), jnp.float32),
            ],
            compiler_params=params,
            name="early_products",
        )(index, outside, inside, first, near_first, second, near_second)
        far_second = sent(far_first, beside)

        def own_and_near(parity, b):
            return b, b ^ (1 + parity)

        def next_and_far(parity, b):
            return b ^ (2 - parity), b ^ 3

        layout, pieces = ((0, 2), (1, 2)), (next_first, far_first, next_second, far_second)
        blocks_of, early_of = next_and_far, own_and_near
    else:
        outside, inside = ends()
        every = lax.all_gather(flat, "blk")
        early = ()
        layout, pieces = ((None, cycle_size),), [every[b] for b in range(cycle_size)]
        blocks_of, early_of = (lambda parity, b: tuple(range(cycle_size))), None
    best = pl.pallas_call(
        functools.partial(
            late_kernel, layout, blocks_of, early_of, block_rows, total_rows, extent
        ),
        in_specs=[in_smem()] * 6 + [in_vmem()] * (3 + len(early) + len(pieces)),
        out_specs=in_vmem(),
        out_shape=jax.ShapeDtypeStruct((total_rows, videos), jnp.float32),
        compiler_params=params,
        name="late_products",
    )(*scalars, index, outside, inside, *early, *pieces)
    step = 1
    while step < time_size:
        other = sent(best, lambda t, b: (t ^ step, b))
        if 2 * step < time_size:
            best = jnp.maximum(best, other)
        step *= 2
    return pl.pallas_call(
        score_kernel,
        in_specs=[in_smem()] + [in_vmem()] * 2,
        out_specs=in_vmem(),
        out_shape=jax.ShapeDtypeStruct((1, query_lengths.shape[0], videos), jnp.float32),
        compiler_params=params,
        name="clip_scores",
    )(query_lengths, best, other)


def solution(mesh):
    placed = (
        P("blk", None, None),
        P("blk", None, "tm", None),
        P(),
        P(),
        P(),
        P(),
        P("blk", None),
        P(),
    )
    return jax.shard_map(
        shards, mesh=mesh, in_specs=placed, out_specs=P("blk", None, None), check_vma=False
    )
```

time: 150 us -> 42.2 us (0.28)
  waiting for transfers between devices: 74.3 us -> 12.9 us
  blocking collectives: 25.9 us -> 0 us
  matrix products: 23.3 us -> 0 us
  Pallas kernels: 0 us -> 6.4 us
  other arithmetic: 8.28 us -> 2.66 us
  starting transfers between devices: 11.9 us -> 16.5 us
    ppermute x7 -> x11, waiting for transfers between devices: 74.3 us -> 12.9 us  [sent(): return lax.ppermute(x, ('tm', 'blk'), pairs)]
    pmax x1 -> x0, blocking collectives: 25.9 us -> none  [shards(): global_max = lax.pmax(video_table, 'tm')]
    dot_general x13 -> x0, matrix products: 23.3 us -> none  [the longest x4 20.1 us: frame_similarity(): lax.dot_general(block.reshape(row_count * regions, feature_width), index_...]
    pallas_call x0 -> x3, Pallas kernels: none -> 6.4 us  [the longest x1 3.55 us: shards(): pl.pallas_call(functools.partial(late_kernel, layout, blocks_of, early_of...]
    ppermute x7 -> x11, starting transfers between devices: 11.9 us -> 16.5 us  [sent(): return lax.ppermute(x, ('tm', 'blk'), pairs)]
    slice x3 -> x0, local copies, waits for them, and re-layouts: 2.96 us -> none  [the longest x2 2.88 us: padded(): last = lax.slice_in_dim(x, length - width, length, axis=dim)]
    unnamed x47 -> x0, other arithmetic: 2.87 us -> none
    select_n x6 -> x2, other arithmetic: 0.05 us -> 2.66 us  [the longest x1 1.52 us: ends(): inner_side = jnp.where(odd, head, tail)]
  transfers between devices with their start and end apart: 7 -> 11, of which waited for: 4 -> 7; matrix products, arithmetic and copies ran while one was open for 9% -> 5% of each run, Pallas kernels for 0% -> 4%
where the time goes in v1:
time: 42.2 us; the launch traced here: 42 us
  starting transfers between devices  16.5 us (39%)
  waiting for transfers between devices  12.9 us (31%)
  Pallas kernels  6.4 us (15%)
  local copies, waits for them, and re-layouts  2.69 us (6%)
  other arithmetic  2.66 us (6%)
  between operations  0.8 us (2%)
    ppermute x11, starting transfers between devices, sent(): return lax.ppermute(x, ('tm', 'blk'), pairs)  16.5 us
    ppermute x11, waiting for transfers between devices, sent(): return lax.ppermute(x, ('tm', 'blk'), pairs)  12.9 us
    pallas_call x1, Pallas kernels, shards(): pl.pallas_call(functools.partial(late_kernel, layout, blocks_of, early_of...  3.55 us
    unnamed x12, local copies, waits for them, and re-layouts  2.27 us
    pallas_call x1, Pallas kernels, shards(): pl.pallas_call(functools.partial(early_kernel, ((1, 2), (0, 2))), in_spec...  1.7 us
    select_n x1, other arithmetic, ends(): inner_side = jnp.where(odd, head, tail)  1.52 us
    pallas_call x1, Pallas kernels, shards(): pl.pallas_call(score_kernel, in_specs=[in_smem()] + [in_vmem()] * 2, out_...  1.15 us
    select_n x1, other arithmetic, shards(): second = jnp.where(odd, flat[:, half:], flat[:, :half])  1.13 us
  transfers between devices with their start and end apart: 11, of which 7 were waited for; matrix products, arithmetic and copies ran while one was open for 5% of the time, Pallas kernels for 4%

profile of v1, /device:TPU:0, one launch (start us, length us, event | category | flops | bytes accessed | tf_op | source)
XLA Modules:
  0.0 42.0 jit_solution(16482546766492907071)
XLA Ops:
  0.0 1.1 %broadcast_select_fusion = (bf16[72,1920]{1,0:T(8,128)(2,1)S(1)}, bf16[72,1920]{1,0:T(8,128)(2,1)S(1)}) fusion(pred[]{:T(512)S(6)} %eq.5, bf16[72,3840]{1,0:T(8,128)(2,1)} %bitcast.7), kind=kLoop, calls=%fused_computation | loop fusion | flops 276480 | bytes 1105921 | tf_op jit(solution)/shard_map/jit(_where)/select_n | solution.py:261
  1.2 3.0 %collective-permute-start.2 = (bf16[72,1920]{1,0:T(8,128)(2,1)S(1)}, bf16[72,1920]{1,0:T(8,128)(2,1)S(1)}, u32[]{:S(2)}, u32[]{:S(2)}) collective-permute-start(bf16[72,1920]{1,0:T(8,128)(2,1)S(1)} %get-tuple-element.12.refs_0_), channel_id=1, source_target_pairs={{1,0},{0,1},{3,2},{2,3},{6,4},{7,5},{4,6},{5,7},{9,8},{8,9},{11,10... | collective-permute-start | bytes 829448 | tf_op jit(solution)/shard_map/ppermute | solution.py:241
  4.2 0.1 collective-permute-start.3
  4.2 4.4 %collective-permute-done.2.refs_1_ = bf16[72,1920]{1,0:T(8,128)(2,1)S(1)} collective-permute-done((bf16[72,1920]{1,0:T(8,128)(2,1)S(1)}, bf16[72,1920]{1,0:T(8,128)(2,1)S(1)}, u32[]{:S(2)}, u32[]{:S(2)}) %collective-permute-start.2) | collective-permute-done | bytes 276512 | tf_op jit(solution)/shard_map/ppermute | solution.py:241
  8.7 0.6 %collective-permute-start.5 = (bf16[72,1920]{1,0:T(8,128)(2,1)S(1)}, bf16[72,1920]{1,0:T(8,128)(2,1)S(1)}, u32[]{:S(2)}, u32[]{:S(2)}) collective-permute-start(bf16[72,1920]{1,0:T(8,128)(2,1)S(1)} %collective-permute-done.2.refs_1_), channel_id=1, source_target_pairs={{5,0},{4,1},{7,2},{6,3},{2,4},{3,5},{0,6},{1,7},{13,8},{12,9},{15,... | collective-permute-start | bytes 829448 | tf_op jit(solution)/shard_map/ppermute | solution.py:241
  9.3 1.5 %collective-permute-start.4 = (bf16[72,1920]{1,0:T(8,128)(2,1)S(1)}, bf16[72,1920]{1,0:T(8,128)(2,1)S(1)}, u32[]{:S(2)}, u32[]{:S(2)}) collective-permute-start(bf16[72,1920]{1,0:T(8,128)(2,1)S(1)} %collective-permute-done.2.refs_1_), channel_id=1, source_target_pairs={{4,0},{5,1},{6,2},{7,3},{0,4},{1,5},{2,6},{3,7},{12,8},{13,9},{14,... | collective-permute-start | bytes 829448 | tf_op jit(solution)/shard_map/ppermute | solution.py:241
  10.8 0.8 %collective-permute-done.3.refs_3_ = bf16[72,1920]{1,0:T(8,128)(2,1)S(1)} collective-permute-done((bf16[72,1920]{1,0:T(8,128)(2,1)S(1)}, bf16[72,1920]{1,0:T(8,128)(2,1)S(1)}, u32[]{:S(2)}, u32[]{:S(2)}) %collective-permute-start.3) | collective-permute-done | bytes 276512 | tf_op jit(solution)/shard_map/ppermute | solution.py:241
  11.6 0.0 collective-permute-start.6
  11.6 3.0 %collective-permute-done.5.refs_3_ = bf16[72,1920]{1,0:T(8,128)(2,1)S(1)} collective-permute-done((bf16[72,1920]{1,0:T(8,128)(2,1)S(1)}, bf16[72,1920]{1,0:T(8,128)(2,1)S(1)}, u32[]{:S(2)}, u32[]{:S(2)}) %collective-permute-start.5) | collective-permute-done | bytes 276512 | tf_op jit(solution)/shard_map/ppermute | solution.py:241
  14.6 0.4 %collective-permute-start.7 = (bf16[72,1920]{1,0:T(8,128)(2,1)S(1)}, bf16[72,1920]{1,0:T(8,128)(2,1)S(1)}, u32[]{:S(2)}, u32[]{:S(2)}) collective-permute-start(bf16[72,1920]{1,0:T(8,128)(2,1)S(1)} %collective-permute-done.5.refs_3_), channel_id=1, source_target_pairs={{4,0},{5,1},{6,2},{7,3},{0,4},{1,5},{2,6},{3,7},{12,8},{13,9},{14,... | collective-permute-start | bytes 829448 | tf_op jit(solution)/shard_map/ppermute | solution.py:241
  15.0 1.5 %broadcast_select_fusion.2 = (bf16[9,2,3840]{2,1,0:T(2,128)(2,1)S(1)}, bf16[9,2,3840]{2,1,0:T(2,128)(2,1)S(1)}) fusion(pred[]{:T(512)S(6)} %eq.5, bf16[9,64,3840]{2,1,0:T(8,128)(2,1)} %bitcast.4), kind=kLoop, calls=%fused_computation.2 | loop fusion | flops 138240 | bytes 552961 | tf_op jit(solution)/shard_map/jit(_where)/select_n | solution.py:253
  16.6 0.2 select_n.40
  16.8 0.7 %collective-permute-start = (bf16[18,3840]{1,0:T(8,128)(2,1)S(1)}, bf16[18,3840]{1,0:T(8,128)(2,1)S(1)}, u32[]{:S(2)}, u32[]{:S(2)}) collective-permute-start(bf16[18,3840]{1,0:T(8,128)(2,1)S(1)} %select_n.40), channel_id=1, source_target_pairs={{8,4},{9,5},{10,6},{11,7},{4,8},{5,9},{6,10},{7,11},{16,12},{17,13... | collective-permute-start | bytes 414728 | tf_op jit(solution)/shard_map/ppermute | solution.py:241
  17.5 0.2 select_n.42
  17.7 3.2 %collective-permute-start.1 = (bf16[18,3840]{1,0:T(8,128)(2,1)S(1)}, bf16[18,3840]{1,0:T(8,128)(2,1)S(1)}, u32[]{:S(2)}, u32[]{:S(2)}) collective-permute-start(bf16[18,3840]{1,0:T(8,128)(2,1)S(1)} %select_n.42), channel_id=1, source_target_pairs={{4,0},{5,1},{6,2},{7,3},{0,4},{1,5},{2,6},{3,7},{12,8},{13,9},{14,... | collective-permute-start | bytes 414728 | tf_op jit(solution)/shard_map/ppermute | solution.py:241
  21.6 0.0 collective-permute-done.outside_ref
  21.6 0.4 collective-permute-done.1.inside_ref
  22.0 2.3 %copy-done = bf16[1,9,64,3840]{3,2,1,0:T(8,128)(2,1)S(1)} copy-done((bf16[1,9,64,3840]{3,2,1,0:T(8,128)(2,1)S(1)}, bf16[1,9,64,3840]{3,2,1,0:T(8,128)(2,1)}, u32[]{:S(2)}) %copy-start) | copy-done | bytes 4423704
  24.2 1.7 %early_products.1 = (f32[64,144]{1,0:T(8,128)S(1)}, f32[8,144]{1,0:T(8,128)S(1)}) custom-call(bf16[9,64,3840]{2,1,0:T(8,128)(2,1)S(1)} %bitcast.5, bf16[18,3840]{1,0:T(8,128)(2,1)S(1)} %collective-permute-done.outside_ref, bf16[18,3840]{1,0:T(8,128)(2,1)S(1)} %collective-permute-done.1.inside_ref, bf16[72,1920]{1,0:T(8,128)(2,1)S(1)} %get-tuple-element.12.refs_0_, ...), custom_call_target="tpu_custom_call" | custom-call | tf_op jit(solution)/shard_map/early_products/pallas_call | solution.py:275
  25.9 0.0 collective-permute-done.4.refs_2_
  25.9 0.0 collective-permute-done.6.refs_4_
  25.9 0.0 collective-permute-done.7.refs_5_
  26.0 0.0 copy-done.3
  26.0 0.0 copy-done.4
  26.0 3.6 %late_products.1 = f32[32,8]{1,0:T(8,128)S(1)} custom-call(s32[1,8]{1,0:T(1,128)S(1)} %copy-done.4, s32[4]{0:T(128)S(1)} %copy-done.3, f32[16,9]{1,0:T(8,128)S(1)} %copy-done.1, f32[16]{0:T(128)S(1)} %copy-done.5, f32[16,9]{1,0:T(8,128)S(1)} %copy-done.2, f32[1]{0:T(128)S(6)} %copy.9.bias_two_ref, bf16[9,64,3840]{2,1,0:T(8,128)(2,1)S(1)} %bitcast.6, ...), custom_call_target="tpu_custom_call" | custom-call | tf_op jit(solution)/shard_map/late_products/pallas_call | solution.py:302
  29.6 1.9 %collective-permute-start.8 = (f32[32,8]{1,0:T(8,128)S(1)}, f32[32,8]{1,0:T(8,128)S(1)}, u32[]{:S(2)}, u32[]{:S(2)}) collective-permute-start(f32[32,8]{1,0:T(8,128)S(1)} %late_products.1), channel_id=1, source_target_pairs={{4,0},{5,1},{6,2},{7,3},{0,4},{1,5},{2,6},{3,7},{12,8},{13,9},{14,... | collective-permute-start | bytes 3080 | tf_op jit(solution)/shard_map/ppermute | solution.py:241
  31.5 0.8 %collective-permute-done.8 = f32[32,8]{1,0:T(8,128)S(1)} collective-permute-done((f32[32,8]{1,0:T(8,128)S(1)}, f32[32,8]{1,0:T(8,128)S(1)}, u32[]{:S(2)}, u32[]{:S(2)}) %collective-permute-start.8) | collective-permute-done | bytes 1056 | tf_op jit(solution)/shard_map/ppermute | solution.py:241
  32.4 2.0 %collective-permute-start.9 = (f32[32,8]{1,0:T(8,128)S(1)}, f32[32,8]{1,0:T(8,128)S(1)}, u32[]{:S(2)}, u32[]{:S(2)}) collective-permute-start(f32[32,8]{1,0:T(8,128)S(1)} %max.6), channel_id=1, source_target_pairs={{8,0},{9,1},{10,2},{11,3},{12,4},{13,5},{14,6},{15,7},{0,8},{1,9},... | collective-permute-start | bytes 3080 | tf_op jit(solution)/shard_map/ppermute | solution.py:241
  34.4 1.7 %collective-permute-done.9 = f32[32,8]{1,0:T(8,128)S(1)} collective-permute-done((f32[32,8]{1,0:T(8,128)S(1)}, f32[32,8]{1,0:T(8,128)S(1)}, u32[]{:S(2)}, u32[]{:S(2)}) %collective-permute-start.9) | collective-permute-done | bytes 1056 | tf_op jit(solution)/shard_map/ppermute | solution.py:241
  36.1 3.0 %collective-permute-start.10 = (f32[32,8]{1,0:T(8,128)S(1)}, f32[32,8]{1,0:T(8,128)S(1)}, u32[]{:S(2)}, u32[]{:S(2)}) collective-permute-start(f32[32,8]{1,0:T(8,128)S(1)} %max.7.refs_0_), channel_id=1, source_target_pairs={{16,0},{17,1},{18,2},{19,3},{20,4},{21,5},{22,6},{23,7},{24,8},{25... | collective-permute-start | bytes 3080 | tf_op jit(solution)/shard_map/ppermute | solution.py:241
  39.1 1.7 %collective-permute-done.10.refs_1_ = f32[32,8]{1,0:T(8,128)S(1)} collective-permute-done((f32[32,8]{1,0:T(8,128)S(1)}, f32[32,8]{1,0:T(8,128)S(1)}, u32[]{:S(2)}, u32[]{:S(2)}) %collective-permute-start.10) | collective-permute-done | bytes 1056 | tf_op jit(solution)/shard_map/ppermute | solution.py:241
  40.8 1.1 %clip_scores.1 = f32[1,4,8]{2,1,0:T(4,128)} custom-call(s32[4]{0:T(128)S(1)} %copy-done.3, f32[32,8]{1,0:T(8,128)S(1)} %max.7.refs_0_, f32[32,8]{1,0:T(8,128)S(1)} %collective-permute-done.10.refs_1_), custom_call_target="tpu_custom_call" | custom-call | tf_op jit(solution)/shard_map/clip_scores/pallas_call | solution.py:318
  (11 shorter events, 0.0 us)
Async XLA Ops:
  0.0 26.0 %copy-start.3 = (s32[4]{0:T(128)S(1)}, s32[4]{0:T(128)}, u32[]{:S(2)}) copy-start(s32[4]{0:T(128)} %clip_ref.3) | copy-start | bytes 52
  0.0 26.0 %copy-start.4 = (s32[1,8]{1,0:T(1,128)S(1)}, s32[1,8]{1,0:T(1,128)}, u32[]{:S(2)}) copy-start(s32[1,8]{1,0:T(1,128)} %video_ref.1) | copy-start | bytes 100
  0.0 26.0 %copy-start.1 = (f32[16,9]{1,0:T(8,128)S(1)}, f32[16,9]{1,0:T(8,128)}, u32[]{:S(2)}) copy-start(f32[16,9]{1,0:T(8,128)} %one_ref.1) | copy-start | bytes 1732
  0.0 26.0 %copy-start.5 = (f32[16]{0:T(128)S(1)}, f32[16]{0:T(128)}, u32[]{:S(2)}) copy-start(f32[16]{0:T(128)} %bias_one_ref.1) | copy-start | bytes 196
  0.0 26.0 %copy-start.2 = (f32[16,9]{1,0:T(8,128)S(1)}, f32[16,9]{1,0:T(8,128)}, u32[]{:S(2)}) copy-start(f32[16,9]{1,0:T(8,128)} %two_ref.1) | copy-start | bytes 1732
  1.2 7.5 %collective-permute-start.2 = (bf16[72,1920]{1,0:T(8,128)(2,1)S(1)}, bf16[72,1920]{1,0:T(8,128)(2,1)S(1)}, u32[]{:S(2)}, u32[]{:S(2)}) collective-permute-start(bf16[72,1920]{1,0:T(8,128)(2,1)S(1)} %get-tuple-element.12.refs_0_), channel_id=1, source_target_pairs={{1,0},{0,1},{3,2},{2,3},{6,4},{7,5},{4,6},{5,7},{9,8},{8,9},{11,10... | collective-permute-start | bytes 829448 | tf_op jit(solution)/shard_map/ppermute | solution.py:241
  4.2 7.5 %collective-permute-start.3 = (bf16[72,1920]{1,0:T(8,128)(2,1)S(1)}, bf16[72,1920]{1,0:T(8,128)(2,1)S(1)}, u32[]{:S(2)}, u32[]{:S(2)}) collective-permute-start(bf16[72,1920]{1,0:T(8,128)(2,1)S(1)} %get-tuple-element.11.refs_2_), channel_id=1, source_target_pairs={{1,0},{0,1},{3,2},{2,3},{6,4},{7,5},{4,6},{5,7},{9,8},{8,9},{11,10... | collective-permute-start | bytes 829448 | tf_op jit(solution)/shard_map/ppermute | solution.py:241
  8.7 6.0 %collective-permute-start.5 = (bf16[72,1920]{1,0:T(8,128)(2,1)S(1)}, bf16[72,1920]{1,0:T(8,128)(2,1)S(1)}, u32[]{:S(2)}, u32[]{:S(2)}) collective-permute-start(bf16[72,1920]{1,0:T(8,128)(2,1)S(1)} %collective-permute-done.2.refs_1_), channel_id=1, source_target_pairs={{5,0},{4,1},{7,2},{6,3},{2,4},{3,5},{0,6},{1,7},{13,8},{12,9},{15,... | collective-permute-start | bytes 829448 | tf_op jit(solution)/shard_map/ppermute | solution.py:241
  9.3 16.6 %collective-permute-start.4 = (bf16[72,1920]{1,0:T(8,128)(2,1)S(1)}, bf16[72,1920]{1,0:T(8,128)(2,1)S(1)}, u32[]{:S(2)}, u32[]{:S(2)}) collective-permute-start(bf16[72,1920]{1,0:T(8,128)(2,1)S(1)} %collective-permute-done.2.refs_1_), channel_id=1, source_target_pairs={{4,0},{5,1},{6,2},{7,3},{0,4},{1,5},{2,6},{3,7},{12,8},{13,9},{14,... | collective-permute-start | bytes 829448 | tf_op jit(solution)/shard_map/ppermute | solution.py:241
  11.6 14.3 %collective-permute-start.6 = (bf16[72,1920]{1,0:T(8,128)(2,1)S(1)}, bf16[72,1920]{1,0:T(8,128)(2,1)S(1)}, u32[]{:S(2)}, u32[]{:S(2)}) collective-permute-start(bf16[72,1920]{1,0:T(8,128)(2,1)S(1)} %collective-permute-done.3.refs_3_), channel_id=1, source_target_pairs={{4,0},{5,1},{6,2},{7,3},{0,4},{1,5},{2,6},{3,7},{12,8},{13,9},{14,... | collective-permute-start | bytes 829448 | tf_op jit(solution)/shard_map/ppermute | solution.py:241
  14.6 11.3 %collective-permute-start.7 = (bf16[72,1920]{1,0:T(8,128)(2,1)S(1)}, bf16[72,1920]{1,0:T(8,128)(2,1)S(1)}, u32[]{:S(2)}, u32[]{:S(2)}) collective-permute-start(bf16[72,1920]{1,0:T(8,128)(2,1)S(1)} %collective-permute-done.5.refs_3_), channel_id=1, source_target_pairs={{4,0},{5,1},{6,2},{7,3},{0,4},{1,5},{2,6},{3,7},{12,8},{13,9},{14,... | collective-permute-start | bytes 829448 | tf_op jit(solution)/shard_map/ppermute | solution.py:241
  16.8 4.8 %collective-permute-start = (bf16[18,3840]{1,0:T(8,128)(2,1)S(1)}, bf16[18,3840]{1,0:T(8,128)(2,1)S(1)}, u32[]{:S(2)}, u32[]{:S(2)}) collective-permute-start(bf16[18,3840]{1,0:T(8,128)(2,1)S(1)} %select_n.40), channel_id=1, source_target_pairs={{8,4},{9,5},{10,6},{11,7},{4,8},{5,9},{6,10},{7,11},{16,12},{17,13... | collective-permute-start | bytes 414728 | tf_op jit(solution)/shard_map/ppermute | solution.py:241
  17.7 4.3 %collective-permute-start.1 = (bf16[18,3840]{1,0:T(8,128)(2,1)S(1)}, bf16[18,3840]{1,0:T(8,128)(2,1)S(1)}, u32[]{:S(2)}, u32[]{:S(2)}) collective-permute-start(bf16[18,3840]{1,0:T(8,128)(2,1)S(1)} %select_n.42), channel_id=1, source_target_pairs={{4,0},{5,1},{6,2},{7,3},{0,4},{1,5},{2,6},{3,7},{12,8},{13,9},{14,... | collective-permute-start | bytes 414728 | tf_op jit(solution)/shard_map/ppermute | solution.py:241
  22.0 2.3 %copy-start = (bf16[1,9,64,3840]{3,2,1,0:T(8,128)(2,1)S(1)}, bf16[1,9,64,3840]{3,2,1,0:T(8,128)(2,1)}, u32[]{:S(2)}) copy-start(bf16[1,9,64,3840]{3,2,1,0:T(8,128)(2,1)} %param.9) | copy-start | bytes 13271044
  29.6 2.8 %collective-permute-start.8 = (f32[32,8]{1,0:T(8,128)S(1)}, f32[32,8]{1,0:T(8,128)S(1)}, u32[]{:S(2)}, u32[]{:S(2)}) collective-permute-start(f32[32,8]{1,0:T(8,128)S(1)} %late_products.1), channel_id=1, source_target_pairs={{4,0},{5,1},{6,2},{7,3},{0,4},{1,5},{2,6},{3,7},{12,8},{13,9},{14,... | collective-permute-start | bytes 3080 | tf_op jit(solution)/shard_map/ppermute | solution.py:241
  32.4 3.7 %collective-permute-start.9 = (f32[32,8]{1,0:T(8,128)S(1)}, f32[32,8]{1,0:T(8,128)S(1)}, u32[]{:S(2)}, u32[]{:S(2)}) collective-permute-start(f32[32,8]{1,0:T(8,128)S(1)} %max.6), channel_id=1, source_target_pairs={{8,0},{9,1},{10,2},{11,3},{12,4},{13,5},{14,6},{15,7},{0,8},{1,9},... | collective-permute-start | bytes 3080 | tf_op jit(solution)/shard_map/ppermute | solution.py:241
  36.1 4.7 %collective-permute-start.10 = (f32[32,8]{1,0:T(8,128)S(1)}, f32[32,8]{1,0:T(8,128)S(1)}, u32[]{:S(2)}, u32[]{:S(2)}) collective-permute-start(f32[32,8]{1,0:T(8,128)S(1)} %max.7.refs_0_), channel_id=1, source_target_pairs={{16,0},{17,1},{18,2},{19,3},{20,4},{21,5},{22,6},{23,7},{24,8},{25... | collective-permute-start | bytes 3080 | tf_op jit(solution)/shard_map/ppermute | solution.py:241

commit v2 on v1

v2 whole, which is shorter than its diff:
```python
import functools
import jax
import jax.numpy as jnp
from jax import lax
from jax.experimental import pallas as pl
from jax.experimental.pallas import tpu as pltpu
from jax.sharding import PartitionSpec as P

very_low = -1000000000.0
highest = lax.Precision.HIGHEST
LANES = 128
SUBLANES = 8
EDGE = 8
VMEM_LIMIT = 32 * 1024 * 1024


def inner(a, b, precision=None):
    return lax.dot_general(
        a, b, (((1,), (1,)), ((), ())), precision=precision, preferred_element_type=jnp.float32
    )


def stacked(refs):
    return refs[0][...] if len(refs) == 1 else jnp.concatenate([r[...] for r in refs], axis=0)


def products_of(index_ref, parts):
    regions, frames, _ = index_ref.shape
    total = None
    for first, size, refs in parts:
        rows = index_ref[:, :, pl.ds(first, size)].reshape(regions * frames, size)
        products = inner(rows, stacked(refs))
        total = products if total is None else total + products
    return total


def region_maxima(products, regions):
    return jnp.max(products.reshape(regions, -1, products.shape[1]), axis=0)


def region_mean(maxima, blocks, block_rows, regions, total_rows):
    frames, width = maxima.shape
    table = jnp.concatenate([maxima, jnp.zeros((LANES - frames, width), jnp.float32)], axis=0)
    row = lax.broadcasted_iota(jnp.int32, (total_rows, width), 0)
    lane = lax.broadcasted_iota(jnp.int32, (total_rows, width), 1)
    per_block = regions * block_rows
    picked = jnp.zeros((total_rows, width), jnp.bool_)
    for number, block in enumerate(blocks):
        inside = (lane >= number * per_block) & (lane < (number + 1) * per_block)
        picked = picked | (inside & (row == block * block_rows + lane % block_rows))
    return inner(picked.astype(jnp.float32), table, highest)


def ids_at(lengths, count, positions):
    found = jnp.full(positions.shape, -1, jnp.int32)
    start = jnp.int32(0)
    for k in range(count):
        found = found + (positions >= start).astype(jnp.int32)
        start = start + lengths(k)
    return found


def rolled(x, step, axis):
    return x if step == 0 else pltpu.roll(x, (-step) % x.shape[axis], axis)


def video_ids(video_ref, position, known):
    return jnp.where(known, ids_at(lambda k: video_ref[0, k], video_ref.shape[1], position), -1)


def refine(similar, position, col_ids, clip_ref, one_ref, bias_one_ref, two_ref, bias_two_ref):
    total_rows, _ = shape = similar.shape
    channels = bias_one_ref.shape[0]
    row = lax.broadcasted_iota(jnp.int32, shape, 0)
    row_ids = ids_at(lambda k: clip_ref[k], clip_ref.shape[0], row)
    steps = (-1, 0, 1)
    col_mask = [
        (
            (rolled(col_ids, b, 1) == col_ids)
            & (col_ids >= 0)
            & (rolled(position, b, 1) == position + b)
        ).astype(jnp.float32)
        for b in steps
    ]
    row_mask = [
        (
            (rolled(row_ids, a, 0) == row_ids) & (row + a >= 0) & (row + a < total_rows)
        ).astype(jnp.float32)
        for a in steps
    ]
    across = [rolled(similar, b, 1) * col_mask[b + 1] for b in steps]
    taps = []
    for a in steps:
        for b in steps:
            tap = across[b + 1]
            taps.append(tap if a == 0 else rolled(tap, a, 0) * row_mask[a + 1])
    piece = 2 * SUBLANES
    gathered = [[] for _ in range(9)]
    for top in range(0, total_rows, piece):
        source = [tap[top : top + piece] for tap in taps]
        sums = [None] * 9
        for c in range(channels):
            hidden = one_ref[c, 0] * source[0] + bias_one_ref[c]
            for t in range(1, 9):
                hidden = hidden + one_ref[c, t] * source[t]
            hidden = jnp.maximum(hidden, 0.0)
            for t in range(9):
                term = two_ref[c, t] * hidden
                sums[t] = term if c == 0 else sums[t] + term
        for t in range(9):
            gathered[t].append(sums[t])
    gathered = [jnp.concatenate(parts, axis=0) for parts in gathered]
    refined = jnp.full(shape, bias_two_ref[0], jnp.float32)
    for b in steps:
        column = gathered[3 + b + 1]
        for a in (-1, 1):
            column = column + rolled(gathered[3 * (a + 1) + b + 1], a, 0) * row_mask[a + 1]
        refined = refined + rolled(column, b, 1) * col_mask[b + 1]
    return refined


def video_best(refined, ids, videos, first_lane):
    lane = lax.broadcasted_iota(jnp.int32, (refined.shape[0], LANES), 1)
    best = jnp.full(lane.shape, very_low, jnp.float32)
    for v in range(videos):
        top = jnp.max(jnp.where(ids == v, refined, very_low), axis=1, keepdims=True)
        best = jnp.where(lane == first_lane + v, top, best)
    return best


def message_lanes(time_size, videos):
    table = time_size * EDGE
    lanes = -(-(table + videos) // LANES) * LANES
    assert table // LANES == lanes // LANES - 1
    return table, lanes


def halves(depth, layout):
    half = depth // 2
    parity = lax.axis_index("tm") % 2
    sides = (parity, 1 - parity)
    return [(pl.multiple_of(sides[k] * half, LANES), half, refs) for k, refs in layout]


def own_kernel(index_ref, first_ref, second_ref, maxima_ref):
    parts = halves(index_ref.shape[2], ((1, [first_ref]), (0, [second_ref])))
    maxima_ref[...] = region_maxima(products_of(index_ref, parts), index_ref.shape[0])


def near_kernel(
    block_rows, total_rows, index_ref, first_ref, second_ref, own_ref, similar_ref
):
    regions = index_ref.shape[0]
    parts = halves(index_ref.shape[2], ((1, [first_ref]), (0, [second_ref])))
    near = region_maxima(products_of(index_ref, parts), regions)
    block = lax.axis_index("blk")
    parity = lax.axis_index("tm") % 2
    mean_of = functools.partial(
        region_mean, block_rows=block_rows, regions=regions, total_rows=total_rows
    )
    similar_ref[...] = mean_of(own_ref[...], (block,)) + mean_of(near, (block ^ (1 + parity),))


def half_kernel(index_ref, next_ref, far_ref, products_ref):
    parts = halves(index_ref.shape[2], ((0, [next_ref, far_ref]),))
    products_ref[...] = products_of(index_ref, parts)


def late_kernel(
    count, block_rows, total_rows,
    video_ref, clip_ref, one_ref, bias_one_ref, two_ref, bias_two_ref, index_ref, *refs,
):
    *refs, message_ref = refs
    regions, frames, depth = index_ref.shape
    videos = video_ref.shape[1]
    time_index = lax.axis_index("tm")
    mean_of = functools.partial(
        region_mean, block_rows=block_rows, regions=regions, total_rows=total_rows
    )
    if count:
        products = products_of(index_ref, ((0, depth, refs),))
        similar = mean_of(region_maxima(products, regions), tuple(range(count)))
    else:
        next_ref, far_ref, products_ref, similar_ref = refs
        parts = halves(depth, ((1, [next_ref, far_ref]),))
        products = products_ref[...] + products_of(index_ref, parts)
        parity = time_index % 2
        block = lax.axis_index("blk")
        blocks = (block ^ (2 - parity), block ^ 3)
        similar = similar_ref[...] + mean_of(region_maxima(products, regions), blocks)
    similar = similar * (1.0 / regions)
    lane = lax.broadcasted_iota(jnp.int32, similar.shape, 1)
    place = time_index * frames + lane
    col_ids = video_ids(video_ref, place, lane < frames)
    refined = refine(
        similar, place, col_ids, clip_ref, one_ref, bias_one_ref, two_ref, bias_two_ref
    )
    inner_ids = jnp.where((lane >= 2) & (lane < frames - 2), col_ids, -1)
    table, lanes = message_lanes(lax.axis_size("tm"), videos)
    best = video_best(refined, inner_ids, videos, table % LANES)
    edges = jnp.where(lane < EDGE // 2, similar, rolled(similar, frames - EDGE, 1))
    edges = jnp.where(lane < EDGE, edges, very_low)
    slot = time_index * EDGE
    edges = pltpu.roll(edges, slot % LANES, 1)
    for k in range(lanes // LANES):
        tile = jnp.where(slot // LANES == k, edges, very_low)
        if k == table // LANES:
            tile = jnp.maximum(tile, best)
        message_ref[:, k * LANES : (k + 1) * LANES] = tile


def score_kernel(
    frames, time_size, video_ref, clip_ref, one_ref, bias_one_ref, two_ref, bias_two_ref, *refs
):
    *messages, scores_ref = refs
    message = messages[0][...]
    for other in messages[1:]:
        message = jnp.maximum(message, other[...])
    videos = video_ref.shape[1]
    clips = clip_ref.shape[0]
    table, lanes = message_lanes(time_size, videos)
    edges = message[:, : -(-table // LANES) * LANES]
    lane = lax.broadcasted_iota(jnp.int32, edges.shape, 1)
    within = lane % EDGE
    place = (lane // EDGE) * frames + within + jnp.where(within < EDGE // 2, 0, frames - EDGE)
    col_ids = video_ids(video_ref, place, lane < table)
    refined = refine(
        edges, place, col_ids, clip_ref, one_ref, bias_one_ref, two_ref, bias_two_ref
    )
    outer_ids = jnp.where((within < 2) | (within >= EDGE - 2), col_ids, -1)
    first_lane = table % LANES
    best = video_best(refined, outer_ids, videos, first_lane)
    best = jnp.maximum(best, message[:, lanes - LANES :])
    row = lax.broadcasted_iota(jnp.int32, best.shape, 0)
    row_ids = ids_at(lambda k: clip_ref[k], clips, row)
    for c in range(clips):
        total = jnp.sum(jnp.where(row_ids == c, best, 0.0), axis=0, keepdims=True)
        scores_ref[0, c : c + 1, :] = (
            total[:, first_lane : first_lane + videos] / clip_ref[c].astype(jnp.float32)
        )


def call(kernel, name, out_shape, arrays, scalars=()):
    in_smem = pl.BlockSpec(memory_space=pltpu.SMEM)
    in_vmem = pl.BlockSpec(memory_space=pltpu.VMEM)
    return pl.pallas_call(
        kernel,
        in_specs=[in_smem] * len(scalars) + [in_vmem] * len(arrays),
        out_specs=in_vmem,
        out_shape=out_shape,
        compiler_params=pltpu.CompilerParams(vmem_limit_bytes=VMEM_LIMIT),
        name=name,
    )(*scalars, *arrays)


def shards(
    queries, index_regions, conv_one, bias_one, conv_two, bias_two, index_lengths, query_lengths
):
    cycle_size = lax.axis_size("blk")
    time_size = lax.axis_size("tm")
    block_rows, regions, depth = queries.shape
    total_rows = block_rows * cycle_size
    index = index_regions[0]
    frames = index.shape[1]
    videos = index_lengths.shape[1]
    odd = lax.axis_index("tm") % 2 == 1
    half = depth // 2
    width = regions * block_rows

    def sent(x, source):
        pairs = []
        for t in range(time_size):
            for b in range(cycle_size):
                found = source(t, b)
                if found is not None and 0 <= found[0] < time_size:
                    pairs.append((found[0] * cycle_size + found[1], t * cycle_size + b))
        return lax.ppermute(x, ("tm", "blk"), pairs)

    def beside(t, b):
        return t ^ 1, b

    flat = jnp.swapaxes(queries, 0, 1).reshape(width, depth)
    scalars = (index_lengths, query_lengths, conv_one, bias_one, conv_two, bias_two)
    if cycle_size == 4:
        first = jnp.where(odd, flat[:, :half], flat[:, half:])
        second = jnp.where(odd, flat[:, half:], flat[:, :half])

        def near(t, b):
            return (t, b ^ 1) if t % 2 == 0 else (t, b ^ 2)

        def far(t, b):
            return (t ^ 1, b ^ 1) if t % 2 == 0 else (t ^ 1, b ^ 2)

        near_first = sent(first, near)
        near_second = sent(second, near)
        own = call(
            own_kernel,
            "own_maxima",
            jax.ShapeDtypeStruct((frames, width), jnp.float32),
            (index, first, second),
        )
        near_first, own = lax.optimization_barrier((near_first, own))
        far_first = sent(near_first, far)
        next_first = sent(near_first, beside)
        next_second = sent(near_second, beside)
        similar = call(
            functools.partial(near_kernel, block_rows, total_rows),
            "near_similarity",
            jax.ShapeDtypeStruct((total_rows, LANES), jnp.float32),
            (index, near_first, near_second, own),
        )
        far_first, similar = lax.optimization_barrier((far_first, similar))
        far_second = sent(far_first, beside)
        products = call(
            half_kernel,
            "half_products",
            jax.ShapeDtypeStruct((regions * frames, 2 * width), jnp.float32),
            (index, next_first, far_first),
        )
        count, pieces = 0, (next_second, far_second, products, similar)
    else:
        every = lax.all_gather(flat, "blk")
        count, pieces = cycle_size, [every[b] for b in range(cycle_size)]
    _, lanes = message_lanes(time_size, videos)
    message = call(
        functools.partial(late_kernel, count, block_rows, total_rows),
        "late_similarity",
        jax.ShapeDtypeStruct((total_rows, lanes), jnp.float32),
        (index, *pieces),
        scalars,
    )
    step = 1
    while step < time_size:
        other = sent(message, lambda t, b: (t ^ step, b))
        if 2 * step < time_size:
            message = jnp.maximum(message, other)
        step *= 2
    return call(
        functools.partial(score_kernel, frames, time_size),
        "clip_scores",
        jax.ShapeDtypeStruct((1, query_lengths.shape[0], videos), jnp.float32),
        (message, other),
        scalars,
    )


def solution(mesh):
    placed = (
        P("blk", None, None),
        P("blk", None, "tm", None),
        P(),
        P(),
        P(),
        P(),
        P("blk", None),
        P(),
    )
    return jax.shard_map(
        shards, mesh=mesh, in_specs=placed, out_specs=P("blk", None, None), check_vma=False
    )
```

time: 42.2 us -> 30.8 us (0.73)
  starting transfers between devices: 16.5 us -> 10.5 us
  waiting for transfers between devices: 12.9 us -> 7.68 us
  Pallas kernels: 6.4 us -> 8.25 us
  other arithmetic: 2.66 us -> 1.09 us
    ppermute x11 -> x9, starting transfers between devices: 16.5 us -> 10.5 us  [sent(): return lax.ppermute(x, ('tm', 'blk'), pairs)]
    ppermute x11 -> x9, waiting for transfers between devices: 12.9 us -> 7.68 us  [sent(): return lax.ppermute(x, ('tm', 'blk'), pairs)]
    pallas_call x3 -> x5, Pallas kernels: 6.4 us -> 8.25 us  [call(): pl.pallas_call(kernel, in_specs=[in_smem] * len(scalars) + [in_vmem] * le...]
    select_n x2 -> x1, other arithmetic: 2.66 us -> 1.08 us  [shards(): first = jnp.where(odd, flat[:, :half], flat[:, half:])]
  transfers between devices with their start and end apart: 11 -> 9, of which waited for: 7 -> 6; matrix products, arithmetic and copies ran while one was open for 5% -> 0% of each run, Pallas kernels for 4% -> 12%
where the time goes in v2:
time: 30.8 us; the launch traced here: 30.6 us
  starting transfers between devices  10.5 us (34%)
  Pallas kernels  8.25 us (27%)
  waiting for transfers between devices  7.68 us (25%)
  local copies, waits for them, and re-layouts  2.28 us (7%)
  other arithmetic  1.09 us (4%)
  between operations  0.79 us (3%)
    ppermute x9, starting transfers between devices, sent(): return lax.ppermute(x, ('tm', 'blk'), pairs)  10.5 us
    pallas_call x5, Pallas kernels, call(): pl.pallas_call(kernel, in_specs=[in_smem] * len(scalars) + [in_vmem] * le...  8.25 us
    ppermute x9, waiting for transfers between devices, sent(): return lax.ppermute(x, ('tm', 'blk'), pairs)  7.68 us
    unnamed x12, local copies, waits for them, and re-layouts  2.28 us
    select_n x1, other arithmetic, shards(): first = jnp.where(odd, flat[:, :half], flat[:, half:])  1.08 us
  transfers between devices with their start and end apart: 9, of which 6 were waited for; matrix products, arithmetic and copies ran while one was open for 0% of the time, Pallas kernels for 12%

profile of v2, /device:TPU:0, one launch (start us, length us, event | category | flops | bytes accessed | tf_op | source)
XLA Modules:
  0.0 30.6 jit_solution(4655471386681187406)
XLA Ops:
  0.0 1.1 %broadcast_select_fusion = (bf16[72,1920]{1,0:T(8,128)(2,1)S(1)}, bf16[72,1920]{1,0:T(8,128)(2,1)S(1)}) fusion(pred[]{:T(512)S(6)} %eq.5, bf16[72,3840]{1,0:T(8,128)(2,1)} %bitcast.8), kind=kLoop, calls=%fused_computation | loop fusion | flops 276480 | bytes 1105921 | tf_op jit(solution)/shard_map/jit(_where)/select_n | solution.py:285
  1.1 3.0 %collective-permute-start.2 = (bf16[72,1920]{1,0:T(8,128)(2,1)S(1)}, bf16[72,1920]{1,0:T(8,128)(2,1)S(1)}, u32[]{:S(2)}, u32[]{:S(2)}) collective-permute-start(bf16[72,1920]{1,0:T(8,128)(2,1)S(1)} %get-tuple-element.13.first_ref), channel_id=1, source_target_pairs={{1,0},{0,1},{3,2},{2,3},{6,4},{7,5},{4,6},{5,7},{9,8},{8,9},{11,10... | collective-permute-start | bytes 829448 | tf_op jit(solution)/shard_map/ppermute | solution.py:277
  4.1 0.1 collective-permute-start
  4.2 2.3 %copy-done = bf16[1,9,64,3840]{3,2,1,0:T(8,128)(2,1)S(1)} copy-done((bf16[1,9,64,3840]{3,2,1,0:T(8,128)(2,1)S(1)}, bf16[1,9,64,3840]{3,2,1,0:T(8,128)(2,1)}, u32[]{:S(2)}) %copy-start) | copy-done | bytes 4423704
  6.4 1.3 %own_maxima.1.own_ref = f32[64,72]{1,0:T(8,128)S(1)} custom-call(bf16[9,64,3840]{2,1,0:T(8,128)(2,1)S(1)} %bitcast.4, bf16[72,1920]{1,0:T(8,128)(2,1)S(1)} %get-tuple-element.13.first_ref, bf16[72,1920]{1,0:T(8,128)(2,1)S(1)} %get-tuple-element.14.second_ref), custom_call_target="tpu_custom_call" | custom-call | tf_op jit(solution)/shard_map/own_maxima/pallas_call | solution.py:246
  7.7 0.0 copy-start.1
  7.8 0.0 copy-start.2
  7.8 0.0 copy-start.3
  7.8 0.0 copy-start.4
  7.8 0.0 copy-start.5
  7.8 0.8 %collective-permute-done.2.first_ref = bf16[72,1920]{1,0:T(8,128)(2,1)S(1)} collective-permute-done((bf16[72,1920]{1,0:T(8,128)(2,1)S(1)}, bf16[72,1920]{1,0:T(8,128)(2,1)S(1)}, u32[]{:S(2)}, u32[]{:S(2)}) %collective-permute-start.2) | collective-permute-done | bytes 276512 | tf_op jit(solution)/shard_map/ppermute | solution.py:277
  8.6 0.6 %collective-permute-start.3 = (bf16[72,1920]{1,0:T(8,128)(2,1)S(1)}, bf16[72,1920]{1,0:T(8,128)(2,1)S(1)}, u32[]{:S(2)}, u32[]{:S(2)}) collective-permute-start(bf16[72,1920]{1,0:T(8,128)(2,1)S(1)} %collective-permute-done.2.first_ref), channel_id=1, source_target_pairs={{5,0},{4,1},{7,2},{6,3},{2,4},{3,5},{0,6},{1,7},{13,8},{12,9},{15,... | collective-permute-start | bytes 829448 | tf_op jit(solution)/shard_map/ppermute | solution.py:277
  9.2 1.5 %collective-permute-start.5 = (bf16[72,1920]{1,0:T(8,128)(2,1)S(1)}, bf16[72,1920]{1,0:T(8,128)(2,1)S(1)}, u32[]{:S(2)}, u32[]{:S(2)}) collective-permute-start(bf16[72,1920]{1,0:T(8,128)(2,1)S(1)} %collective-permute-done.2.first_ref), channel_id=1, source_target_pairs={{4,0},{5,1},{6,2},{7,3},{0,4},{1,5},{2,6},{3,7},{12,8},{13,9},{14,... | collective-permute-start | bytes 829448 | tf_op jit(solution)/shard_map/ppermute | solution.py:277
  10.7 0.8 %collective-permute-done.second_ref = bf16[72,1920]{1,0:T(8,128)(2,1)S(1)} collective-permute-done((bf16[72,1920]{1,0:T(8,128)(2,1)S(1)}, bf16[72,1920]{1,0:T(8,128)(2,1)S(1)}, u32[]{:S(2)}, u32[]{:S(2)}) %collective-permute-start) | collective-permute-done | bytes 276512 | tf_op jit(solution)/shard_map/ppermute | solution.py:277
  11.6 0.0 collective-permute-start.1
  11.6 1.7 %near_similarity.1.refs_3_ = f32[32,128]{1,0:T(8,128)S(1)} custom-call(bf16[9,64,3840]{2,1,0:T(8,128)(2,1)S(1)} %bitcast.5, bf16[72,1920]{1,0:T(8,128)(2,1)S(1)} %collective-permute-done.2.first_ref, bf16[72,1920]{1,0:T(8,128)(2,1)S(1)} %collective-permute-done.second_ref, f32[64,72]{1,0:T(8,128)S(1)} %own_maxima.1.own_ref), custom_call_target="tpu_custom_call" | custom-call | tf_op jit(solution)/shard_map/near_similarity/pallas_call | solution.py:246
  13.2 1.3 %collective-permute-done.3.far_ref = bf16[72,1920]{1,0:T(8,128)(2,1)S(1)} collective-permute-done((bf16[72,1920]{1,0:T(8,128)(2,1)S(1)}, bf16[72,1920]{1,0:T(8,128)(2,1)S(1)}, u32[]{:S(2)}, u32[]{:S(2)}) %collective-permute-start.3) | collective-permute-done | bytes 276512 | tf_op jit(solution)/shard_map/ppermute | solution.py:277
  14.5 0.4 %collective-permute-start.4 = (bf16[72,1920]{1,0:T(8,128)(2,1)S(1)}, bf16[72,1920]{1,0:T(8,128)(2,1)S(1)}, u32[]{:S(2)}, u32[]{:S(2)}) collective-permute-start(bf16[72,1920]{1,0:T(8,128)(2,1)S(1)} %collective-permute-done.3.far_ref), channel_id=1, source_target_pairs={{4,0},{5,1},{6,2},{7,3},{0,4},{1,5},{2,6},{3,7},{12,8},{13,9},{14,... | collective-permute-start | bytes 829448 | tf_op jit(solution)/shard_map/ppermute | solution.py:277
  15.6 0.0 collective-permute-done.5.next_ref
  15.6 0.8 %half_products.1.refs_2_ = f32[576,144]{1,0:T(8,128)S(1)} custom-call(bf16[9,64,3840]{2,1,0:T(8,128)(2,1)S(1)} %bitcast.6, bf16[72,1920]{1,0:T(8,128)(2,1)S(1)} %collective-permute-done.5.next_ref, bf16[72,1920]{1,0:T(8,128)(2,1)S(1)} %collective-permute-done.3.far_ref), custom_call_target="tpu_custom_call" | custom-call | tf_op jit(solution)/shard_map/half_products/pallas_call | solution.py:246
  16.4 0.0 collective-permute-done.1.refs_0_
  16.4 0.0 collective-permute-done.4.refs_1_
  16.4 0.0 copy-done.1
  16.4 0.0 copy-done.2
  16.5 2.4 %late_similarity.1 = f32[32,128]{1,0:T(8,128)S(1)} custom-call(s32[1,8]{1,0:T(1,128)S(1)} %copy-done.3, s32[4]{0:T(128)S(1)} %copy-done.4, f32[16,9]{1,0:T(8,128)S(1)} %copy-done.1, f32[16]{0:T(128)S(1)} %copy-done.5, f32[16,9]{1,0:T(8,128)S(1)} %copy-done.2, f32[1]{0:T(128)S(6)} %copy.9.bias_two_ref, bf16[9,64,3840]{2,1,0:T(8,128)(2,1)S(1)} %bitcast.7, ...), custom_call_target="tpu_custom_call" | custom-call | tf_op jit(solution)/shard_map/late_similarity/pallas_call | solution.py:246
  18.9 0.2 collective-permute-start.6
  19.1 1.1 %collective-permute-done.6 = f32[32,128]{1,0:T(8,128)S(1)} collective-permute-done((f32[32,128]{1,0:T(8,128)S(1)}, f32[32,128]{1,0:T(8,128)S(1)}, u32[]{:S(2)}, u32[]{:S(2)}) %collective-permute-start.6) | collective-permute-done | bytes 16416 | tf_op jit(solution)/shard_map/ppermute | solution.py:277
  20.2 1.9 %collective-permute-start.7 = (f32[32,128]{1,0:T(8,128)S(1)}, f32[32,128]{1,0:T(8,128)S(1)}, u32[]{:S(2)}, u32[]{:S(2)}) collective-permute-start(f32[32,128]{1,0:T(8,128)S(1)} %max.6), channel_id=1, source_target_pairs={{8,0},{9,1},{10,2},{11,3},{12,4},{13,5},{14,6},{15,7},{0,8},{1,9},... | collective-permute-start | bytes 49160 | tf_op jit(solution)/shard_map/ppermute | solution.py:277
  22.0 1.9 %collective-permute-done.7 = f32[32,128]{1,0:T(8,128)S(1)} collective-permute-done((f32[32,128]{1,0:T(8,128)S(1)}, f32[32,128]{1,0:T(8,128)S(1)}, u32[]{:S(2)}, u32[]{:S(2)}) %collective-permute-start.7) | collective-permute-done | bytes 16416 | tf_op jit(solution)/shard_map/ppermute | solution.py:277
  23.9 2.9 %collective-permute-start.8 = (f32[32,128]{1,0:T(8,128)S(1)}, f32[32,128]{1,0:T(8,128)S(1)}, u32[]{:S(2)}, u32[]{:S(2)}) collective-permute-start(f32[32,128]{1,0:T(8,128)S(1)} %max.7.refs_0_), channel_id=1, source_target_pairs={{16,0},{17,1},{18,2},{19,3},{20,4},{21,5},{22,6},{23,7},{24,8},{25... | collective-permute-start | bytes 49160 | tf_op jit(solution)/shard_map/ppermute | solution.py:277
  26.8 1.8 %collective-permute-done.8.refs_1_ = f32[32,128]{1,0:T(8,128)S(1)} collective-permute-done((f32[32,128]{1,0:T(8,128)S(1)}, f32[32,128]{1,0:T(8,128)S(1)}, u32[]{:S(2)}, u32[]{:S(2)}) %collective-permute-start.8) | collective-permute-done | bytes 16416 | tf_op jit(solution)/shard_map/ppermute | solution.py:277
  28.6 2.0 %clip_scores.1 = f32[1,4,8]{2,1,0:T(4,128)} custom-call(s32[1,8]{1,0:T(1,128)S(1)} %copy-done.3, s32[4]{0:T(128)S(1)} %copy-done.4, f32[16,9]{1,0:T(8,128)S(1)} %copy-done.1, f32[16]{0:T(128)S(1)} %copy-done.5, f32[16,9]{1,0:T(8,128)S(1)} %copy-done.2, f32[1]{0:T(128)S(6)} %copy.9.bias_two_ref, f32[32,128]{1,0:T(8,128)S(1)} %max.7.refs_0_, ...), custom_call_target="tpu_custom_call" | custom-call | tf_op jit(solution)/shard_map/clip_scores/pallas_call | solution.py:246
  (6 shorter events, 0.0 us)
Async XLA Ops:
  1.1 7.5 %collective-permute-start.2 = (bf16[72,1920]{1,0:T(8,128)(2,1)S(1)}, bf16[72,1920]{1,0:T(8,128)(2,1)S(1)}, u32[]{:S(2)}, u32[]{:S(2)}) collective-permute-start(bf16[72,1920]{1,0:T(8,128)(2,1)S(1)} %get-tuple-element.13.first_ref), channel_id=1, source_target_pairs={{1,0},{0,1},{3,2},{2,3},{6,4},{7,5},{4,6},{5,7},{9,8},{8,9},{11,10... | collective-permute-start | bytes 829448 | tf_op jit(solution)/shard_map/ppermute | solution.py:277
  4.1 7.5 %collective-permute-start = (bf16[72,1920]{1,0:T(8,128)(2,1)S(1)}, bf16[72,1920]{1,0:T(8,128)(2,1)S(1)}, u32[]{:S(2)}, u32[]{:S(2)}) collective-permute-start(bf16[72,1920]{1,0:T(8,128)(2,1)S(1)} %get-tuple-element.14.second_ref), channel_id=1, source_target_pairs={{1,0},{0,1},{3,2},{2,3},{6,4},{7,5},{4,6},{5,7},{9,8},{8,9},{11,10... | collective-permute-start | bytes 829448 | tf_op jit(solution)/shard_map/ppermute | solution.py:277
  4.2 2.3 %copy-start = (bf16[1,9,64,3840]{3,2,1,0:T(8,128)(2,1)S(1)}, bf16[1,9,64,3840]{3,2,1,0:T(8,128)(2,1)}, u32[]{:S(2)}) copy-start(bf16[1,9,64,3840]{3,2,1,0:T(8,128)(2,1)} %param.9) | copy-start | bytes 13271044
  7.7 8.7 %copy-start.1 = (f32[16,9]{1,0:T(8,128)S(1)}, f32[16,9]{1,0:T(8,128)}, u32[]{:S(2)}) copy-start(f32[16,9]{1,0:T(8,128)} %one_ref.3) | copy-start | bytes 1732
  7.8 8.7 %copy-start.2 = (f32[16,9]{1,0:T(8,128)S(1)}, f32[16,9]{1,0:T(8,128)}, u32[]{:S(2)}) copy-start(f32[16,9]{1,0:T(8,128)} %two_ref.3) | copy-start | bytes 1732
  7.8 8.7 %copy-start.3 = (s32[1,8]{1,0:T(1,128)S(1)}, s32[1,8]{1,0:T(1,128)}, u32[]{:S(2)}) copy-start(s32[1,8]{1,0:T(1,128)} %video_ref.3) | copy-start | bytes 100
  7.8 8.7 %copy-start.4 = (s32[4]{0:T(128)S(1)}, s32[4]{0:T(128)}, u32[]{:S(2)}) copy-start(s32[4]{0:T(128)} %clip_ref.3) | copy-start | bytes 52
  7.8 8.7 %copy-start.5 = (f32[16]{0:T(128)S(1)}, f32[16]{0:T(128)}, u32[]{:S(2)}) copy-start(f32[16]{0:T(128)} %bias_one_ref.3) | copy-start | bytes 196
  8.6 6.0 %collective-permute-start.3 = (bf16[72,1920]{1,0:T(8,128)(2,1)S(1)}, bf16[72,1920]{1,0:T(8,128)(2,1)S(1)}, u32[]{:S(2)}, u32[]{:S(2)}) collective-permute-start(bf16[72,1920]{1,0:T(8,128)(2,1)S(1)} %collective-permute-done.2.first_ref), channel_id=1, source_target_pairs={{5,0},{4,1},{7,2},{6,3},{2,4},{3,5},{0,6},{1,7},{13,8},{12,9},{15,... | collective-permute-start | bytes 829448 | tf_op jit(solution)/shard_map/ppermute | solution.py:277
  9.2 6.4 %collective-permute-start.5 = (bf16[72,1920]{1,0:T(8,128)(2,1)S(1)}, bf16[72,1920]{1,0:T(8,128)(2,1)S(1)}, u32[]{:S(2)}, u32[]{:S(2)}) collective-permute-start(bf16[72,1920]{1,0:T(8,128)(2,1)S(1)} %collective-permute-done.2.first_ref), channel_id=1, source_target_pairs={{4,0},{5,1},{6,2},{7,3},{0,4},{1,5},{2,6},{3,7},{12,8},{13,9},{14,... | collective-permute-start | bytes 829448 | tf_op jit(solution)/shard_map/ppermute | solution.py:277
  11.6 4.9 %collective-permute-start.1 = (bf16[72,1920]{1,0:T(8,128)(2,1)S(1)}, bf16[72,1920]{1,0:T(8,128)(2,1)S(1)}, u32[]{:S(2)}, u32[]{:S(2)}) collective-permute-start(bf16[72,1920]{1,0:T(8,128)(2,1)S(1)} %collective-permute-done.second_ref), channel_id=1, source_target_pairs={{4,0},{5,1},{6,2},{7,3},{0,4},{1,5},{2,6},{3,7},{12,8},{13,9},{14,... | collective-permute-start | bytes 829448 | tf_op jit(solution)/shard_map/ppermute | solution.py:277
  14.5 1.9 %collective-permute-start.4 = (bf16[72,1920]{1,0:T(8,128)(2,1)S(1)}, bf16[72,1920]{1,0:T(8,128)(2,1)S(1)}, u32[]{:S(2)}, u32[]{:S(2)}) collective-permute-start(bf16[72,1920]{1,0:T(8,128)(2,1)S(1)} %collective-permute-done.3.far_ref), channel_id=1, source_target_pairs={{4,0},{5,1},{6,2},{7,3},{0,4},{1,5},{2,6},{3,7},{12,8},{13,9},{14,... | collective-permute-start | bytes 829448 | tf_op jit(solution)/shard_map/ppermute | solution.py:277
  18.9 1.2 %collective-permute-start.6 = (f32[32,128]{1,0:T(8,128)S(1)}, f32[32,128]{1,0:T(8,128)S(1)}, u32[]{:S(2)}, u32[]{:S(2)}) collective-permute-start(f32[32,128]{1,0:T(8,128)S(1)} %late_similarity.1), channel_id=1, source_target_pairs={{4,0},{5,1},{6,2},{7,3},{0,4},{1,5},{2,6},{3,7},{12,8},{13,9},{14,... | collective-permute-start | bytes 49160 | tf_op jit(solution)/shard_map/ppermute | solution.py:277
  20.2 3.7 %collective-permute-start.7 = (f32[32,128]{1,0:T(8,128)S(1)}, f32[32,128]{1,0:T(8,128)S(1)}, u32[]{:S(2)}, u32[]{:S(2)}) collective-permute-start(f32[32,128]{1,0:T(8,128)S(1)} %max.6), channel_id=1, source_target_pairs={{8,0},{9,1},{10,2},{11,3},{12,4},{13,5},{14,6},{15,7},{0,8},{1,9},... | collective-permute-start | bytes 49160 | tf_op jit(solution)/shard_map/ppermute | solution.py:277
  23.9 4.6 %collective-permute-start.8 = (f32[32,128]{1,0:T(8,128)S(1)}, f32[32,128]{1,0:T(8,128)S(1)}, u32[]{:S(2)}, u32[]{:S(2)}) collective-permute-start(f32[32,128]{1,0:T(8,128)S(1)} %max.7.refs_0_), channel_id=1, source_target_pairs={{16,0},{17,1},{18,2},{19,3},{20,4},{21,5},{22,6},{23,7},{24,8},{25... | collective-permute-start | bytes 49160 | tf_op jit(solution)/shard_map/ppermute | solution.py:277

commit v3 on v2

v3 whole, which is shorter than its diff:
```python
import functools
import jax
import jax.numpy as jnp
from jax import lax
from jax.experimental import pallas as pl
from jax.experimental.pallas import tpu as pltpu
from jax.sharding import PartitionSpec as P

very_low = -1000000000.0
LANES = 128
SUBLANES = 8
EDGE = 8
VMEM_LIMIT = 32 * 1024 * 1024


def inner(a, b):
    return lax.dot_general(a, b, (((1,), (1,)), ((), ())), preferred_element_type=jnp.float32)


def stacked(refs):
    return refs[0][...] if len(refs) == 1 else jnp.concatenate([r[...] for r in refs], axis=0)


def products_of(index_ref, parts):
    regions, frames, _ = index_ref.shape
    total = None
    for first, size, refs in parts:
        rows = index_ref[:, :, pl.ds(first, size)].reshape(regions * frames, size)
        products = inner(rows, stacked(refs))
        total = products if total is None else total + products
    return total


def region_maxima(products, regions):
    return jnp.max(products.reshape(regions, -1, products.shape[1]), axis=0)


def region_mean(maxima, blocks, block_rows, regions, total_rows):
    frames, width = maxima.shape
    table = jnp.concatenate([maxima, jnp.zeros((LANES - frames, width), jnp.float32)], axis=0)
    row = lax.broadcasted_iota(jnp.int32, (total_rows, width), 0)
    lane = lax.broadcasted_iota(jnp.int32, (total_rows, width), 1)
    per_block = regions * block_rows
    picked = jnp.zeros((total_rows, width), jnp.bool_)
    for number, block in enumerate(blocks):
        inside = (lane >= number * per_block) & (lane < (number + 1) * per_block)
        picked = picked | (inside & (row == block * block_rows + lane % block_rows))
    picked = picked.astype(jnp.bfloat16)
    total = None
    for _ in range(3):
        piece = table.astype(jnp.bfloat16)
        table = table - piece.astype(jnp.float32)
        summed = inner(picked, piece)
        total = summed if total is None else total + summed
    return total


def rolled(x, step, axis):
    return x if step == 0 else pltpu.roll(x, (-step) % x.shape[axis], axis)


def ids_at(lengths_ref, positions):
    found = jnp.full(positions.shape, -1, jnp.int32)
    start = jnp.zeros(positions.shape, jnp.int32)
    for k in range(lengths_ref.shape[1]):
        found = found + (positions >= start).astype(jnp.int32)
        start = start + jnp.broadcast_to(lengths_ref[0:1, k : k + 1], positions.shape)
    return found


def column_rows(video_ref, place, known, counted):
    ids = jnp.where(known, ids_at(video_ref, place), -1)
    rows = [
        ((rolled(ids, b, 1) == ids) & (ids >= 0) & (rolled(place, b, 1) == place + b)).astype(
            jnp.float32
        )
        for b in (-1, 0, 1)
    ]
    rows.append(jnp.where(counted, ids, -1).astype(jnp.float32))
    slot = lax.broadcasted_iota(jnp.int32, place.shape, 0)
    table = rows[3]
    for k in range(3):
        table = jnp.where(slot == k, rows[k], table)
    return table


def tables_kernel(
    frames, time_size, total_rows, video_ref, clip_ref, one_ref, bias_one_ref, two_ref, bias_two_ref,
    weights_ref, rows_ref, inner_ref, outer_ref, lengths_ref,
):
    channels = one_ref.shape[0]
    spread = (channels, LANES)
    for t in range(9):
        at = t * channels
        weights_ref[at : at + channels] = jnp.broadcast_to(one_ref[:, t : t + 1], spread)
        at = (9 + t) * channels
        weights_ref[at : at + channels] = jnp.broadcast_to(two_ref[:, t : t + 1], spread)
    square = (channels, channels)
    diagonal = lax.broadcasted_iota(jnp.int32, square, 0) == lax.broadcasted_iota(jnp.int32, square, 1)
    bias = jnp.where(diagonal, jnp.broadcast_to(bias_one_ref[0:1, :], square), 0.0)
    at = 18 * channels
    weights_ref[at : at + channels] = jnp.broadcast_to(jnp.sum(bias, axis=1, keepdims=True), spread)
    at = 19 * channels
    weights_ref[at : at + SUBLANES] = jnp.broadcast_to(bias_two_ref[0:1, 0:1], (SUBLANES, LANES))

    row = lax.broadcasted_iota(jnp.int32, (total_rows, LANES), 0)
    row_ids = ids_at(clip_ref, row)
    for k, a in enumerate((-1, 1)):
        same = (rolled(row_ids, a, 0) == row_ids) & (row + a >= 0) & (row + a < total_rows)
        rows_ref[k * total_rows : (k + 1) * total_rows] = same.astype(jnp.float32)
    rows_ref[2 * total_rows :] = row_ids.astype(jnp.float32)
    for c in range(clip_ref.shape[1]):
        lengths_ref[c : c + 1] = jnp.broadcast_to(
            clip_ref[0:1, c : c + 1].astype(jnp.float32), (1, LANES)
        )

    lane = lax.broadcasted_iota(jnp.int32, inner_ref.shape, 1)
    place = lax.axis_index("tm") * frames + lane
    inner_ref[...] = column_rows(
        video_ref, place, lane < frames, (lane >= 2) & (lane < frames - 2)
    )
    lane = lax.broadcasted_iota(jnp.int32, outer_ref.shape, 1)
    within = lane % EDGE
    place = (lane // EDGE) * frames + within + jnp.where(within < EDGE // 2, 0, frames - EDGE)
    outer_ref[...] = column_rows(
        video_ref, place, lane < time_size * EDGE, (within < 2) | (within >= EDGE - 2)
    )


def refine(similar, columns_ref, rows_ref, weights_ref):
    total_rows, _ = similar.shape
    channels = weights_ref.shape[0] // 19
    steps = (-1, 0, 1)
    col_mask = [columns_ref[k : k + 1, :] for k in range(3)]
    row_mask = {}
    for k, a in enumerate((-1, 1)):
        mask = rows_ref[k * total_rows : (k + 1) * total_rows, :]
        row_mask[a] = jnp.concatenate([mask] * (similar.shape[1] // LANES), axis=1)
    across = [rolled(similar, b, 1) * col_mask[b + 1] for b in steps]
    taps = []
    for a in steps:
        for b in steps:
            tap = across[b + 1]
            taps.append(tap if a == 0 else rolled(tap, a, 0) * row_mask[a])
    piece = 2 * SUBLANES
    gathered = [[] for _ in range(9)]

    def weight(kind, c):
        one = weights_ref[kind * channels + c : kind * channels + c + 1, :]
        return jnp.concatenate([one] * (similar.shape[1] // LANES), axis=1)

    for top in range(0, total_rows, piece):
        source = [tap[top : top + piece] for tap in taps]
        sums = [None] * 9
        for c in range(channels):
            hidden = weight(0, c) * source[0] + weight(18, c)
            for t in range(1, 9):
                hidden = hidden + weight(t, c) * source[t]
            hidden = jnp.maximum(hidden, 0.0)
            for t in range(9):
                term = weight(9 + t, c) * hidden
                sums[t] = term if c == 0 else sums[t] + term
        for t in range(9):
            gathered[t].append(sums[t])
    gathered = [jnp.concatenate(parts, axis=0) for parts in gathered]
    refined = weight(19, 0)
    for b in steps:
        column = gathered[3 + b + 1]
        for a in (-1, 1):
            column = column + rolled(gathered[3 * (a + 1) + b + 1], a, 0) * row_mask[a]
        refined = refined + rolled(column, b, 1) * col_mask[b + 1]
    return refined


def video_best(refined, columns_ref, videos, first_lane):
    ids = columns_ref[3:4, :]
    lane = lax.broadcasted_iota(jnp.int32, (refined.shape[0], LANES), 1)
    best = jnp.full(lane.shape, very_low, jnp.float32)
    for v in range(videos):
        top = jnp.max(jnp.where(ids == v, refined, very_low), axis=1, keepdims=True)
        best = jnp.where(lane == first_lane + v, top, best)
    return best


def message_lanes(time_size, videos):
    table = time_size * EDGE
    lanes = -(-(table + videos) // LANES) * LANES
    assert table // LANES == lanes // LANES - 1
    return table, lanes


def halves(depth, layout):
    half = depth // 2
    parity = lax.axis_index("tm") % 2
    sides = (parity, 1 - parity)
    return [(pl.multiple_of(sides[k] * half, LANES), half, refs) for k, refs in layout]


def own_kernel(index_ref, first_ref, second_ref, maxima_ref):
    parts = halves(index_ref.shape[2], ((1, [first_ref]), (0, [second_ref])))
    maxima_ref[...] = region_maxima(products_of(index_ref, parts), index_ref.shape[0])


def near_kernel(
    block_rows, total_rows, index_ref, first_ref, second_ref, own_ref, similar_ref
):
    regions = index_ref.shape[0]
    parts = halves(index_ref.shape[2], ((1, [first_ref]), (0, [second_ref])))
    near = region_maxima(products_of(index_ref, parts), regions)
    block = lax.axis_index("blk")
    parity = lax.axis_index("tm") % 2
    mean_of = functools.partial(
        region_mean, block_rows=block_rows, regions=regions, total_rows=total_rows
    )
    similar_ref[...] = mean_of(own_ref[...], (block,)) + mean_of(near, (block ^ (1 + parity),))


def half_kernel(index_ref, next_ref, far_ref, products_ref):
    parts = halves(index_ref.shape[2], ((0, [next_ref, far_ref]),))
    products_ref[...] = products_of(index_ref, parts)


def late_kernel(
    count, block_rows, total_rows, videos, columns_ref, rows_ref, weights_ref, index_ref, *refs
):
    *refs, message_ref = refs
    regions, frames, depth = index_ref.shape
    time_index = lax.axis_index("tm")
    mean_of = functools.partial(
        region_mean, block_rows=block_rows, regions=regions, total_rows=total_rows
    )
    if count:
        products = products_of(index_ref, ((0, depth, refs),))
        similar = mean_of(region_maxima(products, regions), tuple(range(count)))
    else:
        next_ref, far_ref, products_ref, similar_ref = refs
        parts = halves(depth, ((1, [next_ref, far_ref]),))
        products = products_ref[...] + products_of(index_ref, parts)
        parity = time_index % 2
        block = lax.axis_index("blk")
        blocks = (block ^ (2 - parity), block ^ 3)
        similar = similar_ref[...] + mean_of(region_maxima(products, regions), blocks)
    similar = similar * (1.0 / regions)
    lane = lax.broadcasted_iota(jnp.int32, similar.shape, 1)
    refined = refine(similar, columns_ref, rows_ref, weights_ref)
    table, lanes = message_lanes(lax.axis_size("tm"), videos)
    best = video_best(refined, columns_ref, videos, table % LANES)
    edges = jnp.where(lane < EDGE // 2, similar, rolled(similar, frames - EDGE, 1))
    edges = jnp.where(lane < EDGE, edges, very_low)
    slot = time_index * EDGE
    edges = pltpu.roll(edges, slot % LANES, 1)
    for k in range(lanes // LANES):
        tile = jnp.where(slot // LANES == k, edges, very_low)
        if k == table // LANES:
            tile = jnp.maximum(tile, best)
        message_ref[:, k * LANES : (k + 1) * LANES] = tile


def score_kernel(time_size, videos, columns_ref, rows_ref, weights_ref, lengths_ref, *refs):
    *messages, scores_ref = refs
    message = messages[0][...]
    for other in messages[1:]:
        message = jnp.maximum(message, other[...])
    table, lanes = message_lanes(time_size, videos)
    edges = message[:, : columns_ref.shape[1]]
    total_rows = edges.shape[0]
    refined = refine(edges, columns_ref, rows_ref, weights_ref)
    first_lane = table % LANES
    best = video_best(refined, columns_ref, videos, first_lane)
    best = jnp.maximum(best, message[:, lanes - LANES :])
    row_ids = rows_ref[2 * total_rows :, :]
    for c in range(scores_ref.shape[1]):
        total = jnp.sum(jnp.where(row_ids == c, best, 0.0), axis=0, keepdims=True)
        total = total / lengths_ref[c : c + 1, :]
        scores_ref[0, c : c + 1, :] = total[:, first_lane : first_lane + videos]


def call(kernel, name, out_shape, *arrays):
    place = pl.BlockSpec(memory_space=pltpu.VMEM)
    return pl.pallas_call(
        kernel,
        in_specs=[place] * len(arrays),
        out_specs=jax.tree.map(lambda _: place, out_shape),
        out_shape=out_shape,
        compiler_params=pltpu.CompilerParams(vmem_limit_bytes=VMEM_LIMIT),
        name=name,
    )(*arrays)


def wide(*shape):
    return jax.ShapeDtypeStruct(shape, jnp.float32)


def shards(
    queries, index_regions, conv_one, bias_one, conv_two, bias_two, index_lengths, query_lengths
):
    cycle_size = lax.axis_size("blk")
    time_size = lax.axis_size("tm")
    block_rows, regions, depth = queries.shape
    total_rows = block_rows * cycle_size
    index = index_regions[0]
    frames = index.shape[1]
    videos = index_lengths.shape[1]
    odd = lax.axis_index("tm") % 2 == 1
    half = depth // 2
    width = regions * block_rows

    def sent(x, source):
        pairs = []
        for t in range(time_size):
            for b in range(cycle_size):
                found = source(t, b)
                if found is not None and 0 <= found[0] < time_size:
                    pairs.append((found[0] * cycle_size + found[1], t * cycle_size + b))
        return lax.ppermute(x, ("tm", "blk"), pairs)

    def beside(t, b):
        return t ^ 1, b

    flat = jnp.swapaxes(queries, 0, 1).reshape(width, depth)
    clips = query_lengths.shape[0]
    channels = conv_one.shape[0]
    edge_lanes = -(-time_size * EDGE // LANES) * LANES
    weights, rows, inner_columns, outer_columns, lengths = call(
        functools.partial(tables_kernel, frames, time_size, total_rows),
        "tables",
        (
            wide(19 * channels + SUBLANES, LANES),
            wide(3 * total_rows, LANES),
            wide(SUBLANES, LANES),
            wide(SUBLANES, edge_lanes),
            wide(clips, LANES),
        ),
        index_lengths,
        query_lengths.reshape(1, clips),
        conv_one,
        bias_one.reshape(1, channels),
        conv_two,
        bias_two.reshape(1, 1),
    )
    if cycle_size == 4:
        first = jnp.where(odd, flat[:, :half], flat[:, half:])
        second = jnp.where(odd, flat[:, half:], flat[:, :half])

        def near(t, b):
            return (t, b ^ 1) if t % 2 == 0 else (t, b ^ 2)

        def far(t, b):
            return (t ^ 1, b ^ 1) if t % 2 == 0 else (t ^ 1, b ^ 2)

        near_first = sent(first, near)
        near_second = sent(second, near)
        own = call(own_kernel, "own_maxima", wide(frames, width), index, first, second)
        near_first, own, weights = lax.optimization_barrier((near_first, own, weights))
        far_first = sent(near_first, far)
        next_first = sent(near_first, beside)
        next_second = sent(near_second, beside)
        similar = call(
            functools.partial(near_kernel, block_rows, total_rows),
            "near_similarity",
            wide(total_rows, LANES),
            index, near_first, near_second, own,
        )
        far_first, similar = lax.optimization_barrier((far_first, similar))
        far_second = sent(far_first, beside)
        products = call(
            half_kernel,
            "half_products",
            wide(regions * frames, 2 * width),
            index, next_first, far_first,
        )
        count, pieces = 0, (next_second, far_second, products, similar)
    else:
        every = lax.all_gather(flat, "blk")
        count, pieces = cycle_size, [every[b] for b in range(cycle_size)]
    _, lanes = message_lanes(time_size, videos)
    message = call(
        functools.partial(late_kernel, count, block_rows, total_rows, videos),
        "late_similarity",
        wide(total_rows, lanes),
        inner_columns, rows, weights, index, *pieces,
    )
    step = 1
    while step < time_size:
        other = sent(message, lambda t, b: (t ^ step, b))
        if 2 * step < time_size:
            message = jnp.maximum(message, other)
        step *= 2
    return call(
        functools.partial(score_kernel, time_size, videos),
        "clip_scores",
        wide(1, clips, videos),
        outer_columns, rows, weights, lengths, message, other,
    )


def solution(mesh):
    placed = (
        P("blk", None, None),
        P("blk", None, "tm", None),
        P(),
        P(),
        P(),
        P(),
        P("blk", None),
        P(),
    )
    return jax.shard_map(
        shards, mesh=mesh, in_specs=placed, out_specs=P("blk", None, None), check_vma=False
    )
```

time: 30.8 us -> 29 us (0.942)
  Pallas kernels: 8.25 us -> 6.57 us
  waiting for transfers between devices: 7.68 us -> 7.03 us
  starting transfers between devices: 10.5 us -> 11 us
    pallas_call x5 -> x6, Pallas kernels: 8.25 us -> 6.57 us  [call(): pl.pallas_call(kernel, in_specs=[place] * len(arrays), out_specs=jax.tree...]
    ppermute x9, waiting for transfers between devices: 7.68 us -> 7.03 us  [sent(): return lax.ppermute(x, ('tm', 'blk'), pairs)]
    ppermute x9, starting transfers between devices: 10.5 us -> 11 us  [sent(): return lax.ppermute(x, ('tm', 'blk'), pairs)]
    unnamed x12 -> x14, local copies, waits for them, and re-layouts: 2.28 us -> 2.27 us
  transfers between devices with their start and end apart: 9 -> 9, of which waited for: 6 -> 6; matrix products, arithmetic and copies ran while one was open for 0% -> 0% of each run, Pallas kernels for 12% -> 13%
where the time goes in v3:
time: 29 us; the launch traced here: 28.8 us
  starting transfers between devices  11 us (38%)
  waiting for transfers between devices  7.03 us (24%)
  Pallas kernels  6.57 us (23%)
  local copies, waits for them, and re-layouts  2.27 us (8%)
  other arithmetic  1.14 us (4%)
  between operations  0.8 us (3%)
    ppermute x9, starting transfers between devices, sent(): return lax.ppermute(x, ('tm', 'blk'), pairs)  11 us
    ppermute x9, waiting for transfers between devices, sent(): return lax.ppermute(x, ('tm', 'blk'), pairs)  7.03 us
    pallas_call x6, Pallas kernels, call(): pl.pallas_call(kernel, in_specs=[place] * len(arrays), out_specs=jax.tree...  6.57 us
    unnamed x14, local copies, waits for them, and re-layouts  2.27 us
    select_n x1, other arithmetic, shards(): second = jnp.where(odd, flat[:, half:], flat[:, :half])  1.13 us
  transfers between devices with their start and end apart: 9, of which 6 were waited for; matrix products, arithmetic and copies ran while one was open for 0% of the time, Pallas kernels for 13%

profile of v3, /device:TPU:0, one launch (start us, length us, event | category | flops | bytes accessed | tf_op | source)
XLA Modules:
  0.0 28.8 jit_solution(2873206113827837655)
XLA Ops:
  0.0 1.1 %broadcast_select_fusion = (bf16[72,1920]{1,0:T(8,128)(2,1)S(1)}, bf16[72,1920]{1,0:T(8,128)(2,1)S(1)}) fusion(pred[]{:T(512)S(6)} %eq.5, bf16[72,3840]{1,0:T(8,128)(2,1)} %bitcast.14), kind=kLoop, calls=%fused_computation | loop fusion | flops 276480 | bytes 1105921 | tf_op jit(solution)/shard_map/jit(_where)/select_n | solution.py:343
  1.2 3.0 %collective-permute-start = (bf16[72,1920]{1,0:T(8,128)(2,1)S(1)}, bf16[72,1920]{1,0:T(8,128)(2,1)S(1)}, u32[]{:S(2)}, u32[]{:S(2)}) collective-permute-start(bf16[72,1920]{1,0:T(8,128)(2,1)S(1)} %get-tuple-element.26.first_ref), channel_id=1, source_target_pairs={{1,0},{0,1},{3,2},{2,3},{6,4},{7,5},{4,6},{5,7},{9,8},{8,9},{11,10... | collective-permute-start | bytes 829448 | tf_op jit(solution)/shard_map/ppermute | solution.py:315
  4.2 0.1 collective-permute-start.1
  4.2 2.3 %copy-done = bf16[1,9,64,3840]{3,2,1,0:T(8,128)(2,1)S(1)} copy-done((bf16[1,9,64,3840]{3,2,1,0:T(8,128)(2,1)S(1)}, bf16[1,9,64,3840]{3,2,1,0:T(8,128)(2,1)}, u32[]{:S(2)}) %copy-start) | copy-done | bytes 4423704
  6.5 1.3 %own_maxima.1.own_ref = f32[64,72]{1,0:T(8,128)S(1)} custom-call(bf16[9,64,3840]{2,1,0:T(8,128)(2,1)S(1)} %bitcast.8, bf16[72,1920]{1,0:T(8,128)(2,1)S(1)} %get-tuple-element.26.first_ref, bf16[72,1920]{1,0:T(8,128)(2,1)S(1)} %get-tuple-element.25.second_ref), custom_call_target="tpu_custom_call" | custom-call | tf_op jit(solution)/shard_map/own_maxima/pallas_call | solution.py:280
  8.5 0.0 copy-done.5
  8.5 0.0 copy-done.6
  8.5 0.0 copy-done.2
  8.5 0.0 copy-done.3
  8.5 0.0 copy-done.4
  8.5 0.2 tables.1
  8.8 0.0 collective-permute-done.first_ref
  8.8 0.9 %collective-permute-start.3 = (bf16[72,1920]{1,0:T(8,128)(2,1)S(1)}, bf16[72,1920]{1,0:T(8,128)(2,1)S(1)}, u32[]{:S(2)}, u32[]{:S(2)}) collective-permute-start(bf16[72,1920]{1,0:T(8,128)(2,1)S(1)} %collective-permute-done.first_ref), channel_id=1, source_target_pairs={{5,0},{4,1},{7,2},{6,3},{2,4},{3,5},{0,6},{1,7},{13,8},{12,9},{15,... | collective-permute-start | bytes 829448 | tf_op jit(solution)/shard_map/ppermute | solution.py:315
  9.7 1.2 %collective-permute-start.5 = (bf16[72,1920]{1,0:T(8,128)(2,1)S(1)}, bf16[72,1920]{1,0:T(8,128)(2,1)S(1)}, u32[]{:S(2)}, u32[]{:S(2)}) collective-permute-start(bf16[72,1920]{1,0:T(8,128)(2,1)S(1)} %collective-permute-done.first_ref), channel_id=1, source_target_pairs={{4,0},{5,1},{6,2},{7,3},{0,4},{1,5},{2,6},{3,7},{12,8},{13,9},{14,... | collective-permute-start | bytes 829448 | tf_op jit(solution)/shard_map/ppermute | solution.py:315
  10.9 0.7 %collective-permute-done.1.second_ref = bf16[72,1920]{1,0:T(8,128)(2,1)S(1)} collective-permute-done((bf16[72,1920]{1,0:T(8,128)(2,1)S(1)}, bf16[72,1920]{1,0:T(8,128)(2,1)S(1)}, u32[]{:S(2)}, u32[]{:S(2)}) %collective-permute-start.1) | collective-permute-done | bytes 276512 | tf_op jit(solution)/shard_map/ppermute | solution.py:315
  11.6 0.0 collective-permute-start.2
  11.6 0.0 copy-done.1
  11.6 1.5 %near_similarity.1.refs_3_ = f32[32,128]{1,0:T(8,128)S(1)} custom-call(bf16[9,64,3840]{2,1,0:T(8,128)(2,1)S(1)} %bitcast.9, bf16[72,1920]{1,0:T(8,128)(2,1)S(1)} %collective-permute-done.first_ref, bf16[72,1920]{1,0:T(8,128)(2,1)S(1)} %collective-permute-done.1.second_ref, f32[64,72]{1,0:T(8,128)S(1)} %own_maxima.1.own_ref), custom_call_target="tpu_custom_call" | custom-call | tf_op jit(solution)/shard_map/near_similarity/pallas_call | solution.py:280
  13.2 1.6 %collective-permute-done.3.far_ref = bf16[72,1920]{1,0:T(8,128)(2,1)S(1)} collective-permute-done((bf16[72,1920]{1,0:T(8,128)(2,1)S(1)}, bf16[72,1920]{1,0:T(8,128)(2,1)S(1)}, u32[]{:S(2)}, u32[]{:S(2)}) %collective-permute-start.3) | collective-permute-done | bytes 276512 | tf_op jit(solution)/shard_map/ppermute | solution.py:315
  14.8 0.3 %collective-permute-start.4 = (bf16[72,1920]{1,0:T(8,128)(2,1)S(1)}, bf16[72,1920]{1,0:T(8,128)(2,1)S(1)}, u32[]{:S(2)}, u32[]{:S(2)}) collective-permute-start(bf16[72,1920]{1,0:T(8,128)(2,1)S(1)} %collective-permute-done.3.far_ref), channel_id=1, source_target_pairs={{4,0},{5,1},{6,2},{7,3},{0,4},{1,5},{2,6},{3,7},{12,8},{13,9},{14,... | collective-permute-start | bytes 829448 | tf_op jit(solution)/shard_map/ppermute | solution.py:315
  15.1 0.0 collective-permute-done.5.next_ref
  15.1 0.8 %half_products.1.refs_2_ = f32[576,144]{1,0:T(8,128)S(1)} custom-call(bf16[9,64,3840]{2,1,0:T(8,128)(2,1)S(1)} %bitcast.10, bf16[72,1920]{1,0:T(8,128)(2,1)S(1)} %collective-permute-done.5.next_ref, bf16[72,1920]{1,0:T(8,128)(2,1)S(1)} %collective-permute-done.3.far_ref), custom_call_target="tpu_custom_call" | custom-call | tf_op jit(solution)/shard_map/half_products/pallas_call | solution.py:280
  15.9 0.0 collective-permute-done.2.refs_0_
  15.9 0.4 %collective-permute-done.4.refs_1_ = bf16[72,1920]{1,0:T(8,128)(2,1)S(1)} collective-permute-done((bf16[72,1920]{1,0:T(8,128)(2,1)S(1)}, bf16[72,1920]{1,0:T(8,128)(2,1)S(1)}, u32[]{:S(2)}, u32[]{:S(2)}) %collective-permute-start.4) | collective-permute-done | bytes 276512 | tf_op jit(solution)/shard_map/ppermute | solution.py:315
  16.3 1.5 %late_similarity.1 = f32[32,128]{1,0:T(8,128)S(1)} custom-call(f32[8,128]{1,0:T(8,128)S(1)} %get-tuple-element.20.columns_ref, f32[96,128]{1,0:T(8,128)S(1)} %get-tuple-element.16.rows_ref, f32[312,128]{1,0:T(8,128)S(1)} %get-tuple-element.18.weights_ref, bf16[9,64,3840]{2,1,0:T(8,128)(2,1)S(1)} %bitcast.11, ...), custom_call_target="tpu_custom_call" | custom-call | tf_op jit(solution)/shard_map/late_similarity/pallas_call | solution.py:280
  17.9 0.4 %collective-permute-start.6 = (f32[32,128]{1,0:T(8,128)S(1)}, f32[32,128]{1,0:T(8,128)S(1)}, u32[]{:S(2)}, u32[]{:S(2)}) collective-permute-start(f32[32,128]{1,0:T(8,128)S(1)} %late_similarity.1), channel_id=1, source_target_pairs={{4,0},{5,1},{6,2},{7,3},{0,4},{1,5},{2,6},{3,7},{12,8},{13,9},{14,... | collective-permute-start | bytes 49160 | tf_op jit(solution)/shard_map/ppermute | solution.py:315
  18.3 0.8 %collective-permute-done.6 = f32[32,128]{1,0:T(8,128)S(1)} collective-permute-done((f32[32,128]{1,0:T(8,128)S(1)}, f32[32,128]{1,0:T(8,128)S(1)}, u32[]{:S(2)}, u32[]{:S(2)}) %collective-permute-start.6) | collective-permute-done | bytes 16416 | tf_op jit(solution)/shard_map/ppermute | solution.py:315
  19.1 2.0 %collective-permute-start.7 = (f32[32,128]{1,0:T(8,128)S(1)}, f32[32,128]{1,0:T(8,128)S(1)}, u32[]{:S(2)}, u32[]{:S(2)}) collective-permute-start(f32[32,128]{1,0:T(8,128)S(1)} %max.6), channel_id=1, source_target_pairs={{8,0},{9,1},{10,2},{11,3},{12,4},{13,5},{14,6},{15,7},{0,8},{1,9},... | collective-permute-start | bytes 49160 | tf_op jit(solution)/shard_map/ppermute | solution.py:315
  21.2 1.7 %collective-permute-done.7 = f32[32,128]{1,0:T(8,128)S(1)} collective-permute-done((f32[32,128]{1,0:T(8,128)S(1)}, f32[32,128]{1,0:T(8,128)S(1)}, u32[]{:S(2)}, u32[]{:S(2)}) %collective-permute-start.7) | collective-permute-done | bytes 16416 | tf_op jit(solution)/shard_map/ppermute | solution.py:315
  22.9 3.0 %collective-permute-start.8 = (f32[32,128]{1,0:T(8,128)S(1)}, f32[32,128]{1,0:T(8,128)S(1)}, u32[]{:S(2)}, u32[]{:S(2)}) collective-permute-start(f32[32,128]{1,0:T(8,128)S(1)} %max.7.refs_0_), channel_id=1, source_target_pairs={{16,0},{17,1},{18,2},{19,3},{20,4},{21,5},{22,6},{23,7},{24,8},{25... | collective-permute-start | bytes 49160 | tf_op jit(solution)/shard_map/ppermute | solution.py:315
  25.9 1.7 %collective-permute-done.8.refs_1_ = f32[32,128]{1,0:T(8,128)S(1)} collective-permute-done((f32[32,128]{1,0:T(8,128)S(1)}, f32[32,128]{1,0:T(8,128)S(1)}, u32[]{:S(2)}, u32[]{:S(2)}) %collective-permute-start.8) | collective-permute-done | bytes 16416 | tf_op jit(solution)/shard_map/ppermute | solution.py:315
  27.6 1.2 %clip_scores.1 = f32[1,4,8]{2,1,0:T(4,128)} custom-call(f32[8,128]{1,0:T(8,128)S(1)} %get-tuple-element.15.columns_ref, f32[96,128]{1,0:T(8,128)S(1)} %get-tuple-element.16.rows_ref, f32[312,128]{1,0:T(8,128)S(1)} %get-tuple-element.18.weights_ref, f32[4,128]{1,0:T(4,128)S(1)} %get-tuple-element.19.lengths_ref, f32[32,128]{1,0:T(8,128)S(1)} %max.7.refs_0_, ...), custom_call_target="tpu_custom_call" | custom-call | tf_op jit(solution)/shard_map/clip_scores/pallas_call | solution.py:280
  (9 shorter events, 0.0 us)
Async XLA Ops:
  0.0 8.5 %copy-start.5 = (s32[4]{0:T(128)S(1)}, s32[4]{0:T(128)}, u32[]{:S(2)}) copy-start(s32[4]{0:T(128)} %param.15) | copy-start | bytes 52
  0.0 8.5 %copy-start.6 = (f32[16]{0:T(128)S(1)}, f32[16]{0:T(128)}, u32[]{:S(2)}) copy-start(f32[16]{0:T(128)} %param.11) | copy-start | bytes 196
  0.0 8.5 %copy-start.2 = (f32[16,9]{1,0:T(8,128)S(1)}, f32[16,9]{1,0:T(8,128)}, u32[]{:S(2)}) copy-start(f32[16,9]{1,0:T(8,128)} %one_ref.1) | copy-start | bytes 1732
  0.0 8.5 %copy-start.3 = (f32[16,9]{1,0:T(8,128)S(1)}, f32[16,9]{1,0:T(8,128)}, u32[]{:S(2)}) copy-start(f32[16,9]{1,0:T(8,128)} %two_ref.1) | copy-start | bytes 1732
  0.0 8.5 %copy-start.4 = (s32[1,8]{1,0:T(1,128)S(1)}, s32[1,8]{1,0:T(1,128)}, u32[]{:S(2)}) copy-start(s32[1,8]{1,0:T(1,128)} %video_ref.1) | copy-start | bytes 100
  1.2 7.6 %collective-permute-start = (bf16[72,1920]{1,0:T(8,128)(2,1)S(1)}, bf16[72,1920]{1,0:T(8,128)(2,1)S(1)}, u32[]{:S(2)}, u32[]{:S(2)}) collective-permute-start(bf16[72,1920]{1,0:T(8,128)(2,1)S(1)} %get-tuple-element.26.first_ref), channel_id=1, source_target_pairs={{1,0},{0,1},{3,2},{2,3},{6,4},{7,5},{4,6},{5,7},{9,8},{8,9},{11,10... | collective-permute-start | bytes 829448 | tf_op jit(solution)/shard_map/ppermute | solution.py:315
  4.2 7.5 %collective-permute-start.1 = (bf16[72,1920]{1,0:T(8,128)(2,1)S(1)}, bf16[72,1920]{1,0:T(8,128)(2,1)S(1)}, u32[]{:S(2)}, u32[]{:S(2)}) collective-permute-start(bf16[72,1920]{1,0:T(8,128)(2,1)S(1)} %get-tuple-element.25.second_ref), channel_id=1, source_target_pairs={{1,0},{0,1},{3,2},{2,3},{6,4},{7,5},{4,6},{5,7},{9,8},{8,9},{11,10... | collective-permute-start | bytes 829448 | tf_op jit(solution)/shard_map/ppermute | solution.py:315
  4.2 2.3 %copy-start = (bf16[1,9,64,3840]{3,2,1,0:T(8,128)(2,1)S(1)}, bf16[1,9,64,3840]{3,2,1,0:T(8,128)(2,1)}, u32[]{:S(2)}) copy-start(bf16[1,9,64,3840]{3,2,1,0:T(8,128)(2,1)} %param.9) | copy-start | bytes 13271044
  6.5 5.1 %copy-start.1 = (bf16[1,9,64,3840]{3,2,1,0:T(8,128)(2,1)S(1)}, bf16[1,9,64,3840]{3,2,1,0:T(8,128)(2,1)}, u32[]{:S(2)}) copy-start(bf16[1,9,64,3840]{3,2,1,0:T(8,128)(2,1)} %param.9) | copy-start | bytes 13271044
  8.8 6.0 %collective-permute-start.3 = (bf16[72,1920]{1,0:T(8,128)(2,1)S(1)}, bf16[72,1920]{1,0:T(8,128)(2,1)S(1)}, u32[]{:S(2)}, u32[]{:S(2)}) collective-permute-start(bf16[72,1920]{1,0:T(8,128)(2,1)S(1)} %collective-permute-done.first_ref), channel_id=1, source_target_pairs={{5,0},{4,1},{7,2},{6,3},{2,4},{3,5},{0,6},{1,7},{13,8},{12,9},{15,... | collective-permute-start | bytes 829448 | tf_op jit(solution)/shard_map/ppermute | solution.py:315
  9.7 5.4 %collective-permute-start.5 = (bf16[72,1920]{1,0:T(8,128)(2,1)S(1)}, bf16[72,1920]{1,0:T(8,128)(2,1)S(1)}, u32[]{:S(2)}, u32[]{:S(2)}) collective-permute-start(bf16[72,1920]{1,0:T(8,128)(2,1)S(1)} %collective-permute-done.first_ref), channel_id=1, source_target_pairs={{4,0},{5,1},{6,2},{7,3},{0,4},{1,5},{2,6},{3,7},{12,8},{13,9},{14,... | collective-permute-start | bytes 829448 | tf_op jit(solution)/shard_map/ppermute | solution.py:315
  11.6 4.3 %collective-permute-start.2 = (bf16[72,1920]{1,0:T(8,128)(2,1)S(1)}, bf16[72,1920]{1,0:T(8,128)(2,1)S(1)}, u32[]{:S(2)}, u32[]{:S(2)}) collective-permute-start(bf16[72,1920]{1,0:T(8,128)(2,1)S(1)} %collective-permute-done.1.second_ref), channel_id=1, source_target_pairs={{4,0},{5,1},{6,2},{7,3},{0,4},{1,5},{2,6},{3,7},{12,8},{13,9},{14,... | collective-permute-start | bytes 829448 | tf_op jit(solution)/shard_map/ppermute | solution.py:315
  14.8 1.6 %collective-permute-start.4 = (bf16[72,1920]{1,0:T(8,128)(2,1)S(1)}, bf16[72,1920]{1,0:T(8,128)(2,1)S(1)}, u32[]{:S(2)}, u32[]{:S(2)}) collective-permute-start(bf16[72,1920]{1,0:T(8,128)(2,1)S(1)} %collective-permute-done.3.far_ref), channel_id=1, source_target_pairs={{4,0},{5,1},{6,2},{7,3},{0,4},{1,5},{2,6},{3,7},{12,8},{13,9},{14,... | collective-permute-start | bytes 829448 | tf_op jit(solution)/shard_map/ppermute | solution.py:315
  17.9 1.3 %collective-permute-start.6 = (f32[32,128]{1,0:T(8,128)S(1)}, f32[32,128]{1,0:T(8,128)S(1)}, u32[]{:S(2)}, u32[]{:S(2)}) collective-permute-start(f32[32,128]{1,0:T(8,128)S(1)} %late_similarity.1), channel_id=1, source_target_pairs={{4,0},{5,1},{6,2},{7,3},{0,4},{1,5},{2,6},{3,7},{12,8},{13,9},{14,... | collective-permute-start | bytes 49160 | tf_op jit(solution)/shard_map/ppermute | solution.py:315
  19.1 3.7 %collective-permute-start.7 = (f32[32,128]{1,0:T(8,128)S(1)}, f32[32,128]{1,0:T(8,128)S(1)}, u32[]{:S(2)}, u32[]{:S(2)}) collective-permute-start(f32[32,128]{1,0:T(8,128)S(1)} %max.6), channel_id=1, source_target_pairs={{8,0},{9,1},{10,2},{11,3},{12,4},{13,5},{14,6},{15,7},{0,8},{1,9},... | collective-permute-start | bytes 49160 | tf_op jit(solution)/shard_map/ppermute | solution.py:315
  22.9 4.8 %collective-permute-start.8 = (f32[32,128]{1,0:T(8,128)S(1)}, f32[32,128]{1,0:T(8,128)S(1)}, u32[]{:S(2)}, u32[]{:S(2)}) collective-permute-start(f32[32,128]{1,0:T(8,128)S(1)} %max.7.refs_0_), channel_id=1, source_target_pairs={{16,0},{17,1},{18,2},{19,3},{20,4},{21,5},{22,6},{23,7},{24,8},{25... | collective-permute-start | bytes 49160 | tf_op jit(solution)/shard_map/ppermute | solution.py:315

commit v4 on v3

--- a/solution.py
+++ b/solution.py
@@ -10,6 +10,7 @@
 LANES = 128
 SUBLANES = 8
 EDGE = 8
+QUARTER = 32
 VMEM_LIMIT = 32 * 1024 * 1024
 
 
@@ -212,7 +213,7 @@
     mean_of = functools.partial(
         region_mean, block_rows=block_rows, regions=regions, total_rows=total_rows
     )
-    similar_ref[...] = mean_of(own_ref[...], (block,)) + mean_of(near, (block ^ (1 + parity),))
+    similar_ref[...] = mean_of(own_ref[...], (block,)) + mean_of(near, (block ^ (2 - parity),))
 
 
 def half_kernel(index_ref, next_ref, far_ref, products_ref):
@@ -221,7 +222,8 @@
 
 
 def late_kernel(
-    count, block_rows, total_rows, videos, columns_ref, rows_ref, weights_ref, index_ref, *refs
+    count, block_rows, total_rows, videos, packed,
+    columns_ref, rows_ref, weights_ref, index_ref, *refs,
 ):
     *refs, message_ref = refs
     regions, frames, depth = index_ref.shape
@@ -238,15 +240,25 @@
         products = products_ref[...] + products_of(index_ref, parts)
         parity = time_index % 2
         block = lax.axis_index("blk")
-        blocks = (block ^ (2 - parity), block ^ 3)
+        blocks = (block ^ (1 + parity), block ^ 3)
         similar = similar_ref[...] + mean_of(region_maxima(products, regions), blocks)
     similar = similar * (1.0 / regions)
     lane = lax.broadcasted_iota(jnp.int32, similar.shape, 1)
     refined = refine(similar, columns_ref, rows_ref, weights_ref)
+    edges = jnp.where(lane < EDGE // 2, similar, rolled(similar, frames - EDGE, 1))
+    edges = jnp.where(lane < EDGE, edges, very_low)
+    if packed:
+        best = video_best(refined, columns_ref, videos, 0)
+        whole = jnp.maximum(best, pltpu.roll(edges, EDGE * (1 + time_index % 2), 1))
+        lane = lax.broadcasted_iota(jnp.int32, (SUBLANES, LANES), 1)
+        message = whole[:SUBLANES]
+        for g in range(1, 4):
+            part = pltpu.roll(whole[g * SUBLANES : (g + 1) * SUBLANES], g * QUARTER, 1)
+            message = jnp.where(lane < g * QUARTER, message, part)
+        message_ref[...] = message
+        return
     table, lanes = message_lanes(lax.axis_size("tm"), videos)
     best = video_best(refined, columns_ref, videos, table % LANES)
-    edges = jnp.where(lane < EDGE // 2, similar, rolled(similar, frames - EDGE, 1))
-    edges = jnp.where(lane < EDGE, edges, very_low)
     slot = time_index * EDGE
     edges = pltpu.roll(edges, slot % LANES, 1)
     for k in range(lanes // LANES):
@@ -256,18 +268,40 @@
         message_ref[:, k * LANES : (k + 1) * LANES] = tile
 
 
-def score_kernel(time_size, videos, columns_ref, rows_ref, weights_ref, lengths_ref, *refs):
+def unpacked(pairs, table_lane):
+    together = functools.reduce(jnp.maximum, pairs)
+    lane = lax.broadcasted_iota(jnp.int32, together.shape, 1)
+    mine = lax.axis_index("tm") // 2
+    edges = []
+    table = []
+    for g in range(4):
+        found = jnp.zeros_like(together)
+        for k, pair in enumerate(pairs):
+            target = 2 * EDGE * (mine ^ k)
+            moved = pltpu.roll(pair, (target + LANES - g * QUARTER - EDGE) % LANES, 1)
+            found = jnp.where(lane // (2 * EDGE) == mine ^ k, moved, found)
+        edges.append(found)
+        table.append(rolled(together, g * QUARTER - table_lane, 1))
+    return jnp.concatenate(edges, axis=0), jnp.concatenate(table, axis=0)
+
+
+def score_kernel(
+    time_size, videos, packed, columns_ref, rows_ref, weights_ref, lengths_ref, *refs
+):
     *messages, scores_ref = refs
-    message = messages[0][...]
-    for other in messages[1:]:
-        message = jnp.maximum(message, other[...])
-    table, lanes = message_lanes(time_size, videos)
-    edges = message[:, : columns_ref.shape[1]]
+    messages = [message[...] for message in messages]
+    if packed:
+        messages = [m[k : k + SUBLANES] for m in messages for k in (0, SUBLANES)]
+    first, lanes = message_lanes(time_size, videos)
+    first_lane = first % LANES
+    if packed:
+        edges, table = unpacked(messages, first_lane)
+    else:
+        message = functools.reduce(jnp.maximum, messages)
+        edges, table = message[:, : columns_ref.shape[1]], message[:, lanes - LANES :]
     total_rows = edges.shape[0]
     refined = refine(edges, columns_ref, rows_ref, weights_ref)
-    first_lane = table % LANES
-    best = video_best(refined, columns_ref, videos, first_lane)
-    best = jnp.maximum(best, message[:, lanes - LANES :])
+    best = jnp.maximum(table, video_best(refined, columns_ref, videos, first_lane))
     row_ids = rows_ref[2 * total_rows :, :]
     for c in range(scores_ref.shape[1]):
         total = jnp.sum(jnp.where(row_ids == c, best, 0.0), axis=0, keepdims=True)
@@ -343,17 +377,18 @@
         second = jnp.where(odd, flat[:, half:], flat[:, :half])
 
         def near(t, b):
-            return (t, b ^ 1) if t % 2 == 0 else (t, b ^ 2)
+            return (t, b ^ 2) if t % 2 == 0 else (t, b ^ 1)
 
         def far(t, b):
-            return (t ^ 1, b ^ 1) if t % 2 == 0 else (t ^ 1, b ^ 2)
+            return (t ^ 1, b ^ 2) if t % 2 == 0 else (t ^ 1, b ^ 1)
 
         near_first = sent(first, near)
         near_second = sent(second, near)
         own = call(own_kernel, "own_maxima", wide(frames, width), index, first, second)
-        near_first, own, weights = lax.optimization_barrier((near_first, own, weights))
+        near_first, own = lax.optimization_barrier((near_first, own))
         far_first = sent(near_first, far)
         next_first = sent(near_first, beside)
+        near_second, weights = lax.optimization_barrier((near_second, weights))
         next_second = sent(near_second, beside)
         similar = call(
             functools.partial(near_kernel, block_rows, total_rows),
@@ -373,24 +408,33 @@
     else:
         every = lax.all_gather(flat, "blk")
         count, pieces = cycle_size, [every[b] for b in range(cycle_size)]
-    _, lanes = message_lanes(time_size, videos)
+    packed = time_size == 8 and total_rows == 4 * SUBLANES and videos <= EDGE
+    shape = (SUBLANES, LANES) if packed else (total_rows, message_lanes(time_size, videos)[1])
     message = call(
-        functools.partial(late_kernel, count, block_rows, total_rows, videos),
+        functools.partial(late_kernel, count, block_rows, total_rows, videos, packed),
         "late_similarity",
-        wide(total_rows, lanes),
+        wide(*shape),
         inner_columns, rows, weights, index, *pieces,
     )
-    step = 1
-    while step < time_size:
-        other = sent(message, lambda t, b: (t ^ step, b))
-        if 2 * step < time_size:
-            message = jnp.maximum(message, other)
-        step *= 2
+
+    def swapped(step):
+        return sent(message, lambda t, b: (t ^ step, b))
+
+    if packed:
+        message = jnp.maximum(message, swapped(1))
+        message = jnp.concatenate([message, swapped(2)])
+        messages = [message, swapped(4)]
+    else:
+        step = 1
+        while step < time_size:
+            messages = [message, swapped(step)]
+            message = jnp.maximum(*messages)
+            step *= 2
     return call(
-        functools.partial(score_kernel, time_size, videos),
+        functools.partial(score_kernel, time_size, videos, packed),
         "clip_scores",
         wide(1, clips, videos),
-        outer_columns, rows, weights, lengths, message, other,
+        outer_columns, rows, weights, lengths, *messages,
     )
 
 

time: 29 us -> 28.8 us (level)
  waiting for transfers between devices: 7.03 us -> 6.48 us
  starting transfers between devices: 11 us -> 11.3 us
    ppermute x9, waiting for transfers between devices: 7.03 us -> 6.48 us  [sent(): return lax.ppermute(x, ('tm', 'blk'), pairs)]
where the time goes in v4:
time: 28.8 us; the launch traced here: 28.6 us
  starting transfers between devices  11.3 us (39%)
  Pallas kernels  6.68 us (23%)
  waiting for transfers between devices  6.48 us (22%)
  local copies, waits for them, and re-layouts  2.27 us (8%)
  other arithmetic  1.14 us (4%)
  between operations  0.75 us (3%)
    ppermute x9, starting transfers between devices, sent(): return lax.ppermute(x, ('tm', 'blk'), pairs)  11.3 us
    pallas_call x6, Pallas kernels, call(): pl.pallas_call(kernel, in_specs=[place] * len(arrays), out_specs=jax.tree...  6.68 us
    ppermute x9, waiting for transfers between devices, sent(): return lax.ppermute(x, ('tm', 'blk'), pairs)  6.48 us
    unnamed x14, local copies, waits for them, and re-layouts  2.27 us
    select_n x1, other arithmetic, shards(): first = jnp.where(odd, flat[:, :half], flat[:, half:])  1.13 us
  transfers between devices with their start and end apart: 9, of which 6 were waited for; matrix products, arithmetic and copies ran while one was open for 0% of the time, Pallas kernels for 13%

profile of v4, /device:TPU:0, one launch (start us, length us, event | category | flops | bytes accessed | tf_op | source)
XLA Modules:
  0.0 28.6 jit_solution(8663029297512928957)
XLA Ops:
  0.0 1.1 %broadcast_select_fusion = (bf16[72,1920]{1,0:T(8,128)(2,1)S(1)}, bf16[72,1920]{1,0:T(8,128)(2,1)S(1)}) fusion(pred[]{:T(512)S(6)} %eq.5, bf16[72,3840]{1,0:T(8,128)(2,1)} %bitcast.14), kind=kLoop, calls=%fused_computation | loop fusion | flops 276480 | bytes 1105921 | tf_op jit(solution)/shard_map/jit(_where)/select_n | solution.py:376
  1.2 3.0 %collective-permute-start.2 = (bf16[72,1920]{1,0:T(8,128)(2,1)S(1)}, bf16[72,1920]{1,0:T(8,128)(2,1)S(1)}, u32[]{:S(2)}, u32[]{:S(2)}) collective-permute-start(bf16[72,1920]{1,0:T(8,128)(2,1)S(1)} %get-tuple-element.27.first_ref), channel_id=1, source_target_pairs={{2,0},{3,1},{0,2},{1,3},{5,4},{4,5},{7,6},{6,7},{10,8},{11,9},{8,1... | collective-permute-start | bytes 829448 | tf_op jit(solution)/shard_map/ppermute | solution.py:349
  4.2 0.1 collective-permute-start
  4.3 2.3 %copy-done = bf16[1,9,64,3840]{3,2,1,0:T(8,128)(2,1)S(1)} copy-done((bf16[1,9,64,3840]{3,2,1,0:T(8,128)(2,1)S(1)}, bf16[1,9,64,3840]{3,2,1,0:T(8,128)(2,1)}, u32[]{:S(2)}) %copy-start) | copy-done | bytes 4423704
  6.5 1.3 %own_maxima.1.own_ref = f32[64,72]{1,0:T(8,128)S(1)} custom-call(bf16[9,64,3840]{2,1,0:T(8,128)(2,1)S(1)} %bitcast.8, bf16[72,1920]{1,0:T(8,128)(2,1)S(1)} %get-tuple-element.27.first_ref, bf16[72,1920]{1,0:T(8,128)(2,1)S(1)} %get-tuple-element.28.second_ref), custom_call_target="tpu_custom_call" | custom-call | tf_op jit(solution)/shard_map/own_maxima/pallas_call | solution.py:314
  7.8 0.9 %collective-permute-done.2.first_ref = bf16[72,1920]{1,0:T(8,128)(2,1)S(1)} collective-permute-done((bf16[72,1920]{1,0:T(8,128)(2,1)S(1)}, bf16[72,1920]{1,0:T(8,128)(2,1)S(1)}, u32[]{:S(2)}, u32[]{:S(2)}) %collective-permute-start.2) | collective-permute-done | bytes 276512 | tf_op jit(solution)/shard_map/ppermute | solution.py:349
  8.7 0.6 %collective-permute-start.3 = (bf16[72,1920]{1,0:T(8,128)(2,1)S(1)}, bf16[72,1920]{1,0:T(8,128)(2,1)S(1)}, u32[]{:S(2)}, u32[]{:S(2)}) collective-permute-start(bf16[72,1920]{1,0:T(8,128)(2,1)S(1)} %collective-permute-done.2.first_ref), channel_id=1, source_target_pairs={{6,0},{7,1},{4,2},{5,3},{1,4},{0,5},{3,6},{2,7},{14,8},{15,9},{12,... | collective-permute-start | bytes 829448 | tf_op jit(solution)/shard_map/ppermute | solution.py:349
  9.9 0.0 copy-done.5
  9.9 0.0 copy-done.6
  9.9 0.0 copy-done.2
  10.0 0.0 copy-done.3
  10.0 0.0 copy-done.4
  10.0 0.2 tables.1
  10.2 1.6 %collective-permute-start.5 = (bf16[72,1920]{1,0:T(8,128)(2,1)S(1)}, bf16[72,1920]{1,0:T(8,128)(2,1)S(1)}, u32[]{:S(2)}, u32[]{:S(2)}) collective-permute-start(bf16[72,1920]{1,0:T(8,128)(2,1)S(1)} %collective-permute-done.2.first_ref), channel_id=1, source_target_pairs={{4,0},{5,1},{6,2},{7,3},{0,4},{1,5},{2,6},{3,7},{12,8},{13,9},{14,... | collective-permute-start | bytes 829448 | tf_op jit(solution)/shard_map/ppermute | solution.py:349
  11.8 0.0 collective-permute-done.second_ref
  11.8 0.1 collective-permute-start.1
  11.9 0.0 copy-done.1
  11.9 1.5 %near_similarity.1.refs_3_ = f32[32,128]{1,0:T(8,128)S(1)} custom-call(bf16[9,64,3840]{2,1,0:T(8,128)(2,1)S(1)} %bitcast.9, bf16[72,1920]{1,0:T(8,128)(2,1)S(1)} %collective-permute-done.2.first_ref, bf16[72,1920]{1,0:T(8,128)(2,1)S(1)} %collective-permute-done.second_ref, f32[64,72]{1,0:T(8,128)S(1)} %own_maxima.1.own_ref), custom_call_target="tpu_custom_call" | custom-call | tf_op jit(solution)/shard_map/near_similarity/pallas_call | solution.py:314
  13.5 1.2 %collective-permute-done.3.far_ref = bf16[72,1920]{1,0:T(8,128)(2,1)S(1)} collective-permute-done((bf16[72,1920]{1,0:T(8,128)(2,1)S(1)}, bf16[72,1920]{1,0:T(8,128)(2,1)S(1)}, u32[]{:S(2)}, u32[]{:S(2)}) %collective-permute-start.3) | collective-permute-done | bytes 276512 | tf_op jit(solution)/shard_map/ppermute | solution.py:349
  14.7 0.4 %collective-permute-start.4 = (bf16[72,1920]{1,0:T(8,128)(2,1)S(1)}, bf16[72,1920]{1,0:T(8,128)(2,1)S(1)}, u32[]{:S(2)}, u32[]{:S(2)}) collective-permute-start(bf16[72,1920]{1,0:T(8,128)(2,1)S(1)} %collective-permute-done.3.far_ref), channel_id=1, source_target_pairs={{4,0},{5,1},{6,2},{7,3},{0,4},{1,5},{2,6},{3,7},{12,8},{13,9},{14,... | collective-permute-start | bytes 829448 | tf_op jit(solution)/shard_map/ppermute | solution.py:349
  15.0 0.0 collective-permute-done.5.next_ref
  15.0 0.8 %half_products.1.refs_2_ = f32[576,144]{1,0:T(8,128)S(1)} custom-call(bf16[9,64,3840]{2,1,0:T(8,128)(2,1)S(1)} %bitcast.10, bf16[72,1920]{1,0:T(8,128)(2,1)S(1)} %collective-permute-done.5.next_ref, bf16[72,1920]{1,0:T(8,128)(2,1)S(1)} %collective-permute-done.3.far_ref), custom_call_target="tpu_custom_call" | custom-call | tf_op jit(solution)/shard_map/half_products/pallas_call | solution.py:314
  15.8 0.0 collective-permute-done.1.refs_0_
  15.8 0.4 %collective-permute-done.4.refs_1_ = bf16[72,1920]{1,0:T(8,128)(2,1)S(1)} collective-permute-done((bf16[72,1920]{1,0:T(8,128)(2,1)S(1)}, bf16[72,1920]{1,0:T(8,128)(2,1)S(1)}, u32[]{:S(2)}, u32[]{:S(2)}) %collective-permute-start.4) | collective-permute-done | bytes 276512 | tf_op jit(solution)/shard_map/ppermute | solution.py:349
  16.2 1.6 %late_similarity.1 = f32[8,128]{1,0:T(8,128)S(1)} custom-call(f32[8,128]{1,0:T(8,128)S(1)} %get-tuple-element.21.columns_ref, f32[96,128]{1,0:T(8,128)S(1)} %get-tuple-element.17.rows_ref, f32[312,128]{1,0:T(8,128)S(1)} %get-tuple-element.19.weights_ref, bf16[9,64,3840]{2,1,0:T(8,128)(2,1)S(1)} %bitcast.11, ...), custom_call_target="tpu_custom_call" | custom-call | tf_op jit(solution)/shard_map/late_similarity/pallas_call | solution.py:314
  17.8 0.4 %collective-permute-start.6 = (f32[8,128]{1,0:T(8,128)S(1)}, f32[8,128]{1,0:T(8,128)S(1)}, u32[]{:S(2)}, u32[]{:S(2)}) collective-permute-start(f32[8,128]{1,0:T(8,128)S(1)} %late_similarity.1), channel_id=1, source_target_pairs={{4,0},{5,1},{6,2},{7,3},{0,4},{1,5},{2,6},{3,7},{12,8},{13,9},{14,... | collective-permute-start | bytes 12296 | tf_op jit(solution)/shard_map/ppermute | solution.py:349
  18.2 0.8 %collective-permute-done.6 = f32[8,128]{1,0:T(8,128)S(1)} collective-permute-done((f32[8,128]{1,0:T(8,128)S(1)}, f32[8,128]{1,0:T(8,128)S(1)}, u32[]{:S(2)}, u32[]{:S(2)}) %collective-permute-start.6) | collective-permute-done | bytes 4128 | tf_op jit(solution)/shard_map/ppermute | solution.py:349
  19.0 2.1 %collective-permute-start.7 = (f32[8,128]{1,0:T(8,128)S(1)}, f32[8,128]{1,0:T(8,128)S(1)}, u32[]{:S(2)}, u32[]{:S(2)}) collective-permute-start(f32[8,128]{1,0:T(8,128)S(1)} %max.3), channel_id=1, source_target_pairs={{8,0},{9,1},{10,2},{11,3},{12,4},{13,5},{14,6},{15,7},{0,8},{1,9},... | collective-permute-start | bytes 12296 | tf_op jit(solution)/shard_map/ppermute | solution.py:349
  21.1 1.6 %collective-permute-done.7 = f32[8,128]{1,0:T(8,128)S(1)} collective-permute-done((f32[8,128]{1,0:T(8,128)S(1)}, f32[8,128]{1,0:T(8,128)S(1)}, u32[]{:S(2)}, u32[]{:S(2)}) %collective-permute-start.7) | collective-permute-done | bytes 4128 | tf_op jit(solution)/shard_map/ppermute | solution.py:349
  22.7 3.0 %collective-permute-start.8 = (f32[16,128]{1,0:T(8,128)S(1)}, f32[16,128]{1,0:T(8,128)S(1)}, u32[]{:S(2)}, u32[]{:S(2)}) collective-permute-start(f32[16,128]{1,0:T(8,128)S(1)} %pad_maximum_fusion.refs_0_), channel_id=1, source_target_pairs={{16,0},{17,1},{18,2},{19,3},{20,4},{21,5},{22,6},{23,7},{24,8},{25... | collective-permute-start | bytes 24584 | tf_op jit(solution)/shard_map/ppermute | solution.py:349
  25.7 1.6 %collective-permute-done.8.refs_1_ = f32[16,128]{1,0:T(8,128)S(1)} collective-permute-done((f32[16,128]{1,0:T(8,128)S(1)}, f32[16,128]{1,0:T(8,128)S(1)}, u32[]{:S(2)}, u32[]{:S(2)}) %collective-permute-start.8) | collective-permute-done | bytes 8224 | tf_op jit(solution)/shard_map/ppermute | solution.py:349
  27.3 1.3 %clip_scores.1 = f32[1,4,8]{2,1,0:T(4,128)} custom-call(f32[8,128]{1,0:T(8,128)S(1)} %get-tuple-element.16.columns_ref, f32[96,128]{1,0:T(8,128)S(1)} %get-tuple-element.17.rows_ref, f32[312,128]{1,0:T(8,128)S(1)} %get-tuple-element.19.weights_ref, f32[4,128]{1,0:T(4,128)S(1)} %get-tuple-element.20.lengths_ref, f32[16,128]{1,0:T(8,128)S(1)} %pad_maximum_fusion.refs_0_, ...), custom_call_target="tpu_custom_call" | custom-call | tf_op jit(solution)/shard_map/clip_scores/pallas_call | solution.py:314
  (9 shorter events, 0.0 us)
Async XLA Ops:
  0.0 9.9 %copy-start.5 = (s32[4]{0:T(128)S(1)}, s32[4]{0:T(128)}, u32[]{:S(2)}) copy-start(s32[4]{0:T(128)} %param.15) | copy-start | bytes 52
  0.0 9.9 %copy-start.6 = (f32[16]{0:T(128)S(1)}, f32[16]{0:T(128)}, u32[]{:S(2)}) copy-start(f32[16]{0:T(128)} %param.11) | copy-start | bytes 196
  0.0 9.9 %copy-start.2 = (f32[16,9]{1,0:T(8,128)S(1)}, f32[16,9]{1,0:T(8,128)}, u32[]{:S(2)}) copy-start(f32[16,9]{1,0:T(8,128)} %one_ref.1) | copy-start | bytes 1732
  0.0 10.0 %copy-start.3 = (f32[16,9]{1,0:T(8,128)S(1)}, f32[16,9]{1,0:T(8,128)}, u32[]{:S(2)}) copy-start(f32[16,9]{1,0:T(8,128)} %two_ref.1) | copy-start | bytes 1732
  0.0 10.0 %copy-start.4 = (s32[1,8]{1,0:T(1,128)S(1)}, s32[1,8]{1,0:T(1,128)}, u32[]{:S(2)}) copy-start(s32[1,8]{1,0:T(1,128)} %video_ref.1) | copy-start | bytes 100
  1.2 7.5 %collective-permute-start.2 = (bf16[72,1920]{1,0:T(8,128)(2,1)S(1)}, bf16[72,1920]{1,0:T(8,128)(2,1)S(1)}, u32[]{:S(2)}, u32[]{:S(2)}) collective-permute-start(bf16[72,1920]{1,0:T(8,128)(2,1)S(1)} %get-tuple-element.27.first_ref), channel_id=1, source_target_pairs={{2,0},{3,1},{0,2},{1,3},{5,4},{4,5},{7,6},{6,7},{10,8},{11,9},{8,1... | collective-permute-start | bytes 829448 | tf_op jit(solution)/shard_map/ppermute | solution.py:349
  4.2 7.6 %collective-permute-start = (bf16[72,1920]{1,0:T(8,128)(2,1)S(1)}, bf16[72,1920]{1,0:T(8,128)(2,1)S(1)}, u32[]{:S(2)}, u32[]{:S(2)}) collective-permute-start(bf16[72,1920]{1,0:T(8,128)(2,1)S(1)} %get-tuple-element.28.second_ref), channel_id=1, source_target_pairs={{2,0},{3,1},{0,2},{1,3},{5,4},{4,5},{7,6},{6,7},{10,8},{11,9},{8,1... | collective-permute-start | bytes 829448 | tf_op jit(solution)/shard_map/ppermute | solution.py:349
  4.3 2.3 %copy-start = (bf16[1,9,64,3840]{3,2,1,0:T(8,128)(2,1)S(1)}, bf16[1,9,64,3840]{3,2,1,0:T(8,128)(2,1)}, u32[]{:S(2)}) copy-start(bf16[1,9,64,3840]{3,2,1,0:T(8,128)(2,1)} %param.9) | copy-start | bytes 13271044
  6.5 5.4 %copy-start.1 = (bf16[1,9,64,3840]{3,2,1,0:T(8,128)(2,1)S(1)}, bf16[1,9,64,3840]{3,2,1,0:T(8,128)(2,1)}, u32[]{:S(2)}) copy-start(bf16[1,9,64,3840]{3,2,1,0:T(8,128)(2,1)} %param.9) | copy-start | bytes 13271044
  8.7 6.0 %collective-permute-start.3 = (bf16[72,1920]{1,0:T(8,128)(2,1)S(1)}, bf16[72,1920]{1,0:T(8,128)(2,1)S(1)}, u32[]{:S(2)}, u32[]{:S(2)}) collective-permute-start(bf16[72,1920]{1,0:T(8,128)(2,1)S(1)} %collective-permute-done.2.first_ref), channel_id=1, source_target_pairs={{6,0},{7,1},{4,2},{5,3},{1,4},{0,5},{3,6},{2,7},{14,8},{15,9},{12,... | collective-permute-start | bytes 829448 | tf_op jit(solution)/shard_map/ppermute | solution.py:349
  10.2 4.8 %collective-permute-start.5 = (bf16[72,1920]{1,0:T(8,128)(2,1)S(1)}, bf16[72,1920]{1,0:T(8,128)(2,1)S(1)}, u32[]{:S(2)}, u32[]{:S(2)}) collective-permute-start(bf16[72,1920]{1,0:T(8,128)(2,1)S(1)} %collective-permute-done.2.first_ref), channel_id=1, source_target_pairs={{4,0},{5,1},{6,2},{7,3},{0,4},{1,5},{2,6},{3,7},{12,8},{13,9},{14,... | collective-permute-start | bytes 829448 | tf_op jit(solution)/shard_map/ppermute | solution.py:349
  11.8 4.0 %collective-permute-start.1 = (bf16[72,1920]{1,0:T(8,128)(2,1)S(1)}, bf16[72,1920]{1,0:T(8,128)(2,1)S(1)}, u32[]{:S(2)}, u32[]{:S(2)}) collective-permute-start(bf16[72,1920]{1,0:T(8,128)(2,1)S(1)} %collective-permute-done.second_ref), channel_id=1, source_target_pairs={{4,0},{5,1},{6,2},{7,3},{0,4},{1,5},{2,6},{3,7},{12,8},{13,9},{14,... | collective-permute-start | bytes 829448 | tf_op jit(solution)/shard_map/ppermute | solution.py:349
  14.7 1.6 %collective-permute-start.4 = (bf16[72,1920]{1,0:T(8,128)(2,1)S(1)}, bf16[72,1920]{1,0:T(8,128)(2,1)S(1)}, u32[]{:S(2)}, u32[]{:S(2)}) collective-permute-start(bf16[72,1920]{1,0:T(8,128)(2,1)S(1)} %collective-permute-done.3.far_ref), channel_id=1, source_target_pairs={{4,0},{5,1},{6,2},{7,3},{0,4},{1,5},{2,6},{3,7},{12,8},{13,9},{14,... | collective-permute-start | bytes 829448 | tf_op jit(solution)/shard_map/ppermute | solution.py:349
  17.8 1.2 %collective-permute-start.6 = (f32[8,128]{1,0:T(8,128)S(1)}, f32[8,128]{1,0:T(8,128)S(1)}, u32[]{:S(2)}, u32[]{:S(2)}) collective-permute-start(f32[8,128]{1,0:T(8,128)S(1)} %late_similarity.1), channel_id=1, source_target_pairs={{4,0},{5,1},{6,2},{7,3},{0,4},{1,5},{2,6},{3,7},{12,8},{13,9},{14,... | collective-permute-start | bytes 12296 | tf_op jit(solution)/shard_map/ppermute | solution.py:349
  19.0 3.6 %collective-permute-start.7 = (f32[8,128]{1,0:T(8,128)S(1)}, f32[8,128]{1,0:T(8,128)S(1)}, u32[]{:S(2)}, u32[]{:S(2)}) collective-permute-start(f32[8,128]{1,0:T(8,128)S(1)} %max.3), channel_id=1, source_target_pairs={{8,0},{9,1},{10,2},{11,3},{12,4},{13,5},{14,6},{15,7},{0,8},{1,9},... | collective-permute-start | bytes 12296 | tf_op jit(solution)/shard_map/ppermute | solution.py:349
  22.7 4.7 %collective-permute-start.8 = (f32[16,128]{1,0:T(8,128)S(1)}, f32[16,128]{1,0:T(8,128)S(1)}, u32[]{:S(2)}, u32[]{:S(2)}) collective-permute-start(f32[16,128]{1,0:T(8,128)S(1)} %pad_maximum_fusion.refs_0_), channel_id=1, source_target_pairs={{16,0},{17,1},{18,2},{19,3},{20,4},{21,5},{22,6},{23,7},{24,8},{25... | collective-permute-start | bytes 24584 | tf_op jit(solution)/shard_map/ppermute | solution.py:349

commit v5 on v4

--- a/solution.py
+++ b/solution.py
@@ -373,8 +373,9 @@
         bias_two.reshape(1, 1),
     )
     if cycle_size == 4:
-        first = jnp.where(odd, flat[:, :half], flat[:, half:])
-        second = jnp.where(odd, flat[:, half:], flat[:, :half])
+        side = jnp.where(odd, half, 0)
+        first = lax.dynamic_slice(flat, (0, half - side), (width, half))
+        second = lax.dynamic_slice(flat, (0, side), (width, half))
 
         def near(t, b):
             return (t, b ^ 2) if t % 2 == 0 else (t, b ^ 1)

time: 28.8 us -> 28.8 us (level)
  other arithmetic: 1.14 us -> 0.01 us
  local copies, waits for them, and re-layouts: 2.27 us -> 3.4 us
    select_n x1 -> x0, other arithmetic: 1.13 us -> none  [shards(): first = jnp.where(odd, flat[:, :half], flat[:, half:])]
    dynamic_slice x0 -> x1, local copies, waits for them, and re-layouts: none -> 1.13 us  [shards(): first = lax.dynamic_slice(flat, (0, half - side), (width, half))]
where the time goes in v5:
time: 28.8 us; the launch traced here: 28.6 us
  starting transfers between devices  11.3 us (39%)
  Pallas kernels  6.68 us (23%)
  waiting for transfers between devices  6.48 us (22%)
  local copies, waits for them, and re-layouts  3.4 us (12%)
  between operations  0.76 us (3%)
    ppermute x9, starting transfers between devices, sent(): return lax.ppermute(x, ('tm', 'blk'), pairs)  11.3 us
    pallas_call x6, Pallas kernels, call(): pl.pallas_call(kernel, in_specs=[place] * len(arrays), out_specs=jax.tree...  6.68 us
    ppermute x9, waiting for transfers between devices, sent(): return lax.ppermute(x, ('tm', 'blk'), pairs)  6.48 us
    unnamed x14, local copies, waits for them, and re-layouts  2.27 us
    dynamic_slice x1, local copies, waits for them, and re-layouts, shards(): first = lax.dynamic_slice(flat, (0, half - side), (width, half))  1.13 us
  transfers between devices with their start and end apart: 9, of which 6 were waited for; matrix products, arithmetic and copies ran while one was open for 0% of the time, Pallas kernels for 13%

profile of v5, /device:TPU:0, one launch (start us, length us, event | category | flops | bytes accessed | tf_op | source)
XLA Modules:
  0.0 28.6 jit_solution(9537724551794123043)
XLA Ops:
  0.0 1.1 %constant_dynamic-slice_fusion = (bf16[72,1920]{1,0:T(8,128)(2,1)S(1)}, bf16[72,1920]{1,0:T(8,128)(2,1)S(1)}) fusion(bf16[72,3840]{1,0:T(8,128)(2,1)} %bitcast.14, s32[]{:T(128)S(6)} %select_n.17, s32[]{:T(128)S(6)} %select_n.16), kind=kLoop, calls=%fused_computation.1 | loop fusion | bytes 1105928 | tf_op jit(solution)/shard_map/dynamic_slice | solution.py:377
  1.2 3.0 %collective-permute-start.2 = (bf16[72,1920]{1,0:T(8,128)(2,1)S(1)}, bf16[72,1920]{1,0:T(8,128)(2,1)S(1)}, u32[]{:S(2)}, u32[]{:S(2)}) collective-permute-start(bf16[72,1920]{1,0:T(8,128)(2,1)S(1)} %get-tuple-element.27.first_ref), channel_id=1, source_target_pairs={{2,0},{3,1},{0,2},{1,3},{5,4},{4,5},{7,6},{6,7},{10,8},{11,9},{8,1... | collective-permute-start | bytes 829448 | tf_op jit(solution)/shard_map/ppermute | solution.py:349
  4.2 0.1 collective-permute-start
  4.3 2.3 %copy-done = bf16[1,9,64,3840]{3,2,1,0:T(8,128)(2,1)S(1)} copy-done((bf16[1,9,64,3840]{3,2,1,0:T(8,128)(2,1)S(1)}, bf16[1,9,64,3840]{3,2,1,0:T(8,128)(2,1)}, u32[]{:S(2)}) %copy-start) | copy-done | bytes 4423704
  6.5 1.3 %own_maxima.1.own_ref = f32[64,72]{1,0:T(8,128)S(1)} custom-call(bf16[9,64,3840]{2,1,0:T(8,128)(2,1)S(1)} %bitcast.8, bf16[72,1920]{1,0:T(8,128)(2,1)S(1)} %get-tuple-element.27.first_ref, bf16[72,1920]{1,0:T(8,128)(2,1)S(1)} %get-tuple-element.28.second_ref), custom_call_target="tpu_custom_call" | custom-call | tf_op jit(solution)/shard_map/own_maxima/pallas_call | solution.py:314
  7.8 0.9 %collective-permute-done.2.first_ref = bf16[72,1920]{1,0:T(8,128)(2,1)S(1)} collective-permute-done((bf16[72,1920]{1,0:T(8,128)(2,1)S(1)}, bf16[72,1920]{1,0:T(8,128)(2,1)S(1)}, u32[]{:S(2)}, u32[]{:S(2)}) %collective-permute-start.2) | collective-permute-done | bytes 276512 | tf_op jit(solution)/shard_map/ppermute | solution.py:349
  8.7 0.6 %collective-permute-start.3 = (bf16[72,1920]{1,0:T(8,128)(2,1)S(1)}, bf16[72,1920]{1,0:T(8,128)(2,1)S(1)}, u32[]{:S(2)}, u32[]{:S(2)}) collective-permute-start(bf16[72,1920]{1,0:T(8,128)(2,1)S(1)} %collective-permute-done.2.first_ref), channel_id=1, source_target_pairs={{6,0},{7,1},{4,2},{5,3},{1,4},{0,5},{3,6},{2,7},{14,8},{15,9},{12,... | collective-permute-start | bytes 829448 | tf_op jit(solution)/shard_map/ppermute | solution.py:349
  9.9 0.0 copy-done.5
  9.9 0.0 copy-done.6
  9.9 0.0 copy-done.2
  10.0 0.0 copy-done.3
  10.0 0.0 copy-done.4
  10.0 0.2 tables.1
  10.2 1.6 %collective-permute-start.5 = (bf16[72,1920]{1,0:T(8,128)(2,1)S(1)}, bf16[72,1920]{1,0:T(8,128)(2,1)S(1)}, u32[]{:S(2)}, u32[]{:S(2)}) collective-permute-start(bf16[72,1920]{1,0:T(8,128)(2,1)S(1)} %collective-permute-done.2.first_ref), channel_id=1, source_target_pairs={{4,0},{5,1},{6,2},{7,3},{0,4},{1,5},{2,6},{3,7},{12,8},{13,9},{14,... | collective-permute-start | bytes 829448 | tf_op jit(solution)/shard_map/ppermute | solution.py:349
  11.8 0.0 collective-permute-done.second_ref
  11.8 0.1 collective-permute-start.1
  11.9 0.0 copy-done.1
  11.9 1.5 %near_similarity.1.refs_3_ = f32[32,128]{1,0:T(8,128)S(1)} custom-call(bf16[9,64,3840]{2,1,0:T(8,128)(2,1)S(1)} %bitcast.9, bf16[72,1920]{1,0:T(8,128)(2,1)S(1)} %collective-permute-done.2.first_ref, bf16[72,1920]{1,0:T(8,128)(2,1)S(1)} %collective-permute-done.second_ref, f32[64,72]{1,0:T(8,128)S(1)} %own_maxima.1.own_ref), custom_call_target="tpu_custom_call" | custom-call | tf_op jit(solution)/shard_map/near_similarity/pallas_call | solution.py:314
  13.5 1.2 %collective-permute-done.3.far_ref = bf16[72,1920]{1,0:T(8,128)(2,1)S(1)} collective-permute-done((bf16[72,1920]{1,0:T(8,128)(2,1)S(1)}, bf16[72,1920]{1,0:T(8,128)(2,1)S(1)}, u32[]{:S(2)}, u32[]{:S(2)}) %collective-permute-start.3) | collective-permute-done | bytes 276512 | tf_op jit(solution)/shard_map/ppermute | solution.py:349
  14.7 0.4 %collective-permute-start.4 = (bf16[72,1920]{1,0:T(8,128)(2,1)S(1)}, bf16[72,1920]{1,0:T(8,128)(2,1)S(1)}, u32[]{:S(2)}, u32[]{:S(2)}) collective-permute-start(bf16[72,1920]{1,0:T(8,128)(2,1)S(1)} %collective-permute-done.3.far_ref), channel_id=1, source_target_pairs={{4,0},{5,1},{6,2},{7,3},{0,4},{1,5},{2,6},{3,7},{12,8},{13,9},{14,... | collective-permute-start | bytes 829448 | tf_op jit(solution)/shard_map/ppermute | solution.py:349
  15.0 0.0 collective-permute-done.5.next_ref
  15.0 0.8 %half_products.1.refs_2_ = f32[576,144]{1,0:T(8,128)S(1)} custom-call(bf16[9,64,3840]{2,1,0:T(8,128)(2,1)S(1)} %bitcast.10, bf16[72,1920]{1,0:T(8,128)(2,1)S(1)} %collective-permute-done.5.next_ref, bf16[72,1920]{1,0:T(8,128)(2,1)S(1)} %collective-permute-done.3.far_ref), custom_call_target="tpu_custom_call" | custom-call | tf_op jit(solution)/shard_map/half_products/pallas_call | solution.py:314
  15.8 0.0 collective-permute-done.1.refs_0_
  15.8 0.4 %collective-permute-done.4.refs_1_ = bf16[72,1920]{1,0:T(8,128)(2,1)S(1)} collective-permute-done((bf16[72,1920]{1,0:T(8,128)(2,1)S(1)}, bf16[72,1920]{1,0:T(8,128)(2,1)S(1)}, u32[]{:S(2)}, u32[]{:S(2)}) %collective-permute-start.4) | collective-permute-done | bytes 276512 | tf_op jit(solution)/shard_map/ppermute | solution.py:349
  16.2 1.6 %late_similarity.1 = f32[8,128]{1,0:T(8,128)S(1)} custom-call(f32[8,128]{1,0:T(8,128)S(1)} %get-tuple-element.21.columns_ref, f32[96,128]{1,0:T(8,128)S(1)} %get-tuple-element.17.rows_ref, f32[312,128]{1,0:T(8,128)S(1)} %get-tuple-element.19.weights_ref, bf16[9,64,3840]{2,1,0:T(8,128)(2,1)S(1)} %bitcast.11, ...), custom_call_target="tpu_custom_call" | custom-call | tf_op jit(solution)/shard_map/late_similarity/pallas_call | solution.py:314
  17.8 0.4 %collective-permute-start.6 = (f32[8,128]{1,0:T(8,128)S(1)}, f32[8,128]{1,0:T(8,128)S(1)}, u32[]{:S(2)}, u32[]{:S(2)}) collective-permute-start(f32[8,128]{1,0:T(8,128)S(1)} %late_similarity.1), channel_id=1, source_target_pairs={{4,0},{5,1},{6,2},{7,3},{0,4},{1,5},{2,6},{3,7},{12,8},{13,9},{14,... | collective-permute-start | bytes 12296 | tf_op jit(solution)/shard_map/ppermute | solution.py:349
  18.2 0.8 %collective-permute-done.6 = f32[8,128]{1,0:T(8,128)S(1)} collective-permute-done((f32[8,128]{1,0:T(8,128)S(1)}, f32[8,128]{1,0:T(8,128)S(1)}, u32[]{:S(2)}, u32[]{:S(2)}) %collective-permute-start.6) | collective-permute-done | bytes 4128 | tf_op jit(solution)/shard_map/ppermute | solution.py:349
  19.0 2.1 %collective-permute-start.7 = (f32[8,128]{1,0:T(8,128)S(1)}, f32[8,128]{1,0:T(8,128)S(1)}, u32[]{:S(2)}, u32[]{:S(2)}) collective-permute-start(f32[8,128]{1,0:T(8,128)S(1)} %max.3), channel_id=1, source_target_pairs={{8,0},{9,1},{10,2},{11,3},{12,4},{13,5},{14,6},{15,7},{0,8},{1,9},... | collective-permute-start | bytes 12296 | tf_op jit(solution)/shard_map/ppermute | solution.py:349
  21.1 1.6 %collective-permute-done.7 = f32[8,128]{1,0:T(8,128)S(1)} collective-permute-done((f32[8,128]{1,0:T(8,128)S(1)}, f32[8,128]{1,0:T(8,128)S(1)}, u32[]{:S(2)}, u32[]{:S(2)}) %collective-permute-start.7) | collective-permute-done | bytes 4128 | tf_op jit(solution)/shard_map/ppermute | solution.py:349
  22.7 3.0 %collective-permute-start.8 = (f32[16,128]{1,0:T(8,128)S(1)}, f32[16,128]{1,0:T(8,128)S(1)}, u32[]{:S(2)}, u32[]{:S(2)}) collective-permute-start(f32[16,128]{1,0:T(8,128)S(1)} %pad_maximum_fusion.refs_0_), channel_id=1, source_target_pairs={{16,0},{17,1},{18,2},{19,3},{20,4},{21,5},{22,6},{23,7},{24,8},{25... | collective-permute-start | bytes 24584 | tf_op jit(solution)/shard_map/ppermute | solution.py:349
  25.7 1.6 %collective-permute-done.8.refs_1_ = f32[16,128]{1,0:T(8,128)S(1)} collective-permute-done((f32[16,128]{1,0:T(8,128)S(1)}, f32[16,128]{1,0:T(8,128)S(1)}, u32[]{:S(2)}, u32[]{:S(2)}) %collective-permute-start.8) | collective-permute-done | bytes 8224 | tf_op jit(solution)/shard_map/ppermute | solution.py:349
  27.3 1.3 %clip_scores.1 = f32[1,4,8]{2,1,0:T(4,128)} custom-call(f32[8,128]{1,0:T(8,128)S(1)} %get-tuple-element.16.columns_ref, f32[96,128]{1,0:T(8,128)S(1)} %get-tuple-element.17.rows_ref, f32[312,128]{1,0:T(8,128)S(1)} %get-tuple-element.19.weights_ref, f32[4,128]{1,0:T(4,128)S(1)} %get-tuple-element.20.lengths_ref, f32[16,128]{1,0:T(8,128)S(1)} %pad_maximum_fusion.refs_0_, ...), custom_call_target="tpu_custom_call" | custom-call | tf_op jit(solution)/shard_map/clip_scores/pallas_call | solution.py:314
  (9 shorter events, 0.0 us)
Async XLA Ops:
  0.0 9.9 %copy-start.5 = (s32[4]{0:T(128)S(1)}, s32[4]{0:T(128)}, u32[]{:S(2)}) copy-start(s32[4]{0:T(128)} %param.15) | copy-start | bytes 52
  0.0 9.9 %copy-start.6 = (f32[16]{0:T(128)S(1)}, f32[16]{0:T(128)}, u32[]{:S(2)}) copy-start(f32[16]{0:T(128)} %param.11) | copy-start | bytes 196
  0.0 9.9 %copy-start.2 = (f32[16,9]{1,0:T(8,128)S(1)}, f32[16,9]{1,0:T(8,128)}, u32[]{:S(2)}) copy-start(f32[16,9]{1,0:T(8,128)} %one_ref.1) | copy-start | bytes 1732
  0.0 10.0 %copy-start.3 = (f32[16,9]{1,0:T(8,128)S(1)}, f32[16,9]{1,0:T(8,128)}, u32[]{:S(2)}) copy-start(f32[16,9]{1,0:T(8,128)} %two_ref.1) | copy-start | bytes 1732
  0.0 10.0 %copy-start.4 = (s32[1,8]{1,0:T(1,128)S(1)}, s32[1,8]{1,0:T(1,128)}, u32[]{:S(2)}) copy-start(s32[1,8]{1,0:T(1,128)} %video_ref.1) | copy-start | bytes 100
  1.2 7.5 %collective-permute-start.2 = (bf16[72,1920]{1,0:T(8,128)(2,1)S(1)}, bf16[72,1920]{1,0:T(8,128)(2,1)S(1)}, u32[]{:S(2)}, u32[]{:S(2)}) collective-permute-start(bf16[72,1920]{1,0:T(8,128)(2,1)S(1)} %get-tuple-element.27.first_ref), channel_id=1, source_target_pairs={{2,0},{3,1},{0,2},{1,3},{5,4},{4,5},{7,6},{6,7},{10,8},{11,9},{8,1... | collective-permute-start | bytes 829448 | tf_op jit(solution)/shard_map/ppermute | solution.py:349
  4.2 7.6 %collective-permute-start = (bf16[72,1920]{1,0:T(8,128)(2,1)S(1)}, bf16[72,1920]{1,0:T(8,128)(2,1)S(1)}, u32[]{:S(2)}, u32[]{:S(2)}) collective-permute-start(bf16[72,1920]{1,0:T(8,128)(2,1)S(1)} %get-tuple-element.28.second_ref), channel_id=1, source_target_pairs={{2,0},{3,1},{0,2},{1,3},{5,4},{4,5},{7,6},{6,7},{10,8},{11,9},{8,1... | collective-permute-start | bytes 829448 | tf_op jit(solution)/shard_map/ppermute | solution.py:349
  4.3 2.3 %copy-start = (bf16[1,9,64,3840]{3,2,1,0:T(8,128)(2,1)S(1)}, bf16[1,9,64,3840]{3,2,1,0:T(8,128)(2,1)}, u32[]{:S(2)}) copy-start(bf16[1,9,64,3840]{3,2,1,0:T(8,128)(2,1)} %param.9) | copy-start | bytes 13271044
  6.5 5.4 %copy-start.1 = (bf16[1,9,64,3840]{3,2,1,0:T(8,128)(2,1)S(1)}, bf16[1,9,64,3840]{3,2,1,0:T(8,128)(2,1)}, u32[]{:S(2)}) copy-start(bf16[1,9,64,3840]{3,2,1,0:T(8,128)(2,1)} %param.9) | copy-start | bytes 13271044
  8.7 6.0 %collective-permute-start.3 = (bf16[72,1920]{1,0:T(8,128)(2,1)S(1)}, bf16[72,1920]{1,0:T(8,128)(2,1)S(1)}, u32[]{:S(2)}, u32[]{:S(2)}) collective-permute-start(bf16[72,1920]{1,0:T(8,128)(2,1)S(1)} %collective-permute-done.2.first_ref), channel_id=1, source_target_pairs={{6,0},{7,1},{4,2},{5,3},{1,4},{0,5},{3,6},{2,7},{14,8},{15,9},{12,... | collective-permute-start | bytes 829448 | tf_op jit(solution)/shard_map/ppermute | solution.py:349
  10.2 4.8 %collective-permute-start.5 = (bf16[72,1920]{1,0:T(8,128)(2,1)S(1)}, bf16[72,1920]{1,0:T(8,128)(2,1)S(1)}, u32[]{:S(2)}, u32[]{:S(2)}) collective-permute-start(bf16[72,1920]{1,0:T(8,128)(2,1)S(1)} %collective-permute-done.2.first_ref), channel_id=1, source_target_pairs={{4,0},{5,1},{6,2},{7,3},{0,4},{1,5},{2,6},{3,7},{12,8},{13,9},{14,... | collective-permute-start | bytes 829448 | tf_op jit(solution)/shard_map/ppermute | solution.py:349
  11.8 4.0 %collective-permute-start.1 = (bf16[72,1920]{1,0:T(8,128)(2,1)S(1)}, bf16[72,1920]{1,0:T(8,128)(2,1)S(1)}, u32[]{:S(2)}, u32[]{:S(2)}) collective-permute-start(bf16[72,1920]{1,0:T(8,128)(2,1)S(1)} %collective-permute-done.second_ref), channel_id=1, source_target_pairs={{4,0},{5,1},{6,2},{7,3},{0,4},{1,5},{2,6},{3,7},{12,8},{13,9},{14,... | collective-permute-start | bytes 829448 | tf_op jit(solution)/shard_map/ppermute | solution.py:349
  14.7 1.6 %collective-permute-start.4 = (bf16[72,1920]{1,0:T(8,128)(2,1)S(1)}, bf16[72,1920]{1,0:T(8,128)(2,1)S(1)}, u32[]{:S(2)}, u32[]{:S(2)}) collective-permute-start(bf16[72,1920]{1,0:T(8,128)(2,1)S(1)} %collective-permute-done.3.far_ref), channel_id=1, source_target_pairs={{4,0},{5,1},{6,2},{7,3},{0,4},{1,5},{2,6},{3,7},{12,8},{13,9},{14,... | collective-permute-start | bytes 829448 | tf_op jit(solution)/shard_map/ppermute | solution.py:349
  17.8 1.2 %collective-permute-start.6 = (f32[8,128]{1,0:T(8,128)S(1)}, f32[8,128]{1,0:T(8,128)S(1)}, u32[]{:S(2)}, u32[]{:S(2)}) collective-permute-start(f32[8,128]{1,0:T(8,128)S(1)} %late_similarity.1), channel_id=1, source_target_pairs={{4,0},{5,1},{6,2},{7,3},{0,4},{1,5},{2,6},{3,7},{12,8},{13,9},{14,... | collective-permute-start | bytes 12296 | tf_op jit(solution)/shard_map/ppermute | solution.py:349
  19.0 3.6 %collective-permute-start.7 = (f32[8,128]{1,0:T(8,128)S(1)}, f32[8,128]{1,0:T(8,128)S(1)}, u32[]{:S(2)}, u32[]{:S(2)}) collective-permute-start(f32[8,128]{1,0:T(8,128)S(1)} %max.3), channel_id=1, source_target_pairs={{8,0},{9,1},{10,2},{11,3},{12,4},{13,5},{14,6},{15,7},{0,8},{1,9},... | collective-permute-start | bytes 12296 | tf_op jit(solution)/shard_map/ppermute | solution.py:349
  22.7 4.7 %collective-permute-start.8 = (f32[16,128]{1,0:T(8,128)S(1)}, f32[16,128]{1,0:T(8,128)S(1)}, u32[]{:S(2)}, u32[]{:S(2)}) collective-permute-start(f32[16,128]{1,0:T(8,128)S(1)} %pad_maximum_fusion.refs_0_), channel_id=1, source_target_pairs={{16,0},{17,1},{18,2},{19,3},{20,4},{21,5},{22,6},{23,7},{24,8},{25... | collective-permute-start | bytes 24584 | tf_op jit(solution)/shard_map/ppermute | solution.py:349
